TPU v7x, 128 devices: a whole 4x4x4 slice. The times are simulated.
128 devices in a mesh: dp: 8 (over z, core), vocab: 16 (over x, y).
Axes of the slice: x: 4, y: 4, z: 4, core: 2. Of those that a mesh axis runs over, the one named last changes fastest.
Arguments:
- hidden: bfloat16 [8, 384, 4096], P('dp', None, 'vocab'), may hold values from -6 to 6
- positions: int32 [8, 384], P('dp'), may hold values from 0 to 383, each once within a row
- targets: int32 [8, 384], P('dp'), may hold values from 0 to 63487
- counts: int32 [8], P('dp'), may hold values from 1 to 384, 1536 in all
- out_weight: bfloat16 [63488, 4096], P(('vocab', 'dp'))
Outputs:
- grad_hidden: bfloat16 [8, 384, 4096], P('dp', None, 'vocab')
Inputs may be any that keep to these rules, and one draw needn't show every extreme that they name: Each row of positions holds every position of its sequence once; its first counts[b] entries are the masked positions of sequence b. The counts sum to 1536; the largest is 384.
All inputs are finite; a program needn't handle non-finite values. No bound on the sum of `counts` on one device may be relied on, other than what follows from the above.
Results may differ from a plain program's by a relative error of at most 0.025.
Values may be sent and summed in bfloat16 or wider, within the bound.
A program may use at most 128 MiB of HBM per device.

v0:
```python
import jax
import jax.numpy as jnp
from jax import lax
from jax.sharding import PartitionSpec as P

smoothing = 0.1


def row_gradients(part_rows, row_targets, row_weights, group_weight, total_vocab):
    whole = lax.all_gather(part_rows, "vocab", axis=1, tiled=True)
    scores = lax.dot_general(
        whole, group_weight, (((1,), (1,)), ((), ())), preferred_element_type=jnp.float32
    )
    block_size = group_weight.shape[0]
    columns = lax.axis_index("vocab") * block_size + jnp.arange(block_size, dtype=jnp.int32)
    top_score = lax.pmax(jnp.max(scores, axis=1), "vocab")
    total = lax.psum(jnp.sum(jnp.exp(scores - top_score[:, None]), axis=1), "vocab")
    probs = jnp.exp(scores - top_score[:, None]) / total[:, None]
    onehot = (columns[None, :] == row_targets[:, None]).astype(jnp.float32)
    dlogits = (
        row_weights[:, None] * (probs - (1.0 - smoothing) * onehot - smoothing / total_vocab)
    ).astype(jnp.bfloat16)
    partial_sum = jnp.dot(dlogits, group_weight, preferred_element_type=jnp.float32)
    return lax.psum_scatter(
        partial_sum.astype(jnp.bfloat16), "vocab", scatter_dimension=1, tiled=True
    )


def local(hidden, positions, targets, counts, out_weight):
    length = positions.shape[1]
    width = hidden.shape[2]
    dp_count = lax.axis_size("dp")
    total_vocab = out_weight.shape[0] * dp_count * lax.axis_size("vocab")
    group_weight = lax.all_gather(out_weight, "dp", axis=0, tiled=True)
    count = counts[0]
    entries = jnp.arange(length, dtype=jnp.int32)
    live = entries < count
    place = positions[0]
    rows = hidden[0][place]
    row_targets = targets[0][place]
    row_weights = jnp.where(live, jnp.float32(length) / count.astype(jnp.float32), jnp.float32(0.0))
    row_grads = row_gradients(rows, row_targets, row_weights, group_weight, total_vocab)
    result = jnp.zeros((1, length, width), jnp.bfloat16)
    return result.at[0, place].set(row_grads)


def solution(mesh):
    return jax.shard_map(
        local,
        mesh=mesh,
        in_specs=(
            P("dp", None, "vocab"),
            P("dp", None),
            P("dp", None),
            P("dp"),
            P(("vocab", "dp"), None),
        ),
        out_specs=P("dp", None, "vocab"),
        check_vma=False,
    )
```

profile of v0, /device:TPU:1, one launch (start us, length us, event | category | flops | bytes accessed | tf_op | source)
XLA Modules:
  0.0 424.1 jit_solution(9136545475463998702)
XLA Ops:
  6.5 0.0 copy-start
  6.5 0.0 all-gather.6.cloned.1.call-start
  6.5 0.7 fusion.12
  7.3 0.2 copy-done
  7.5 2.5 gather_fusion
  10.0 0.0 all-gather.6.cloned.1.call-update
  10.1 0.0 all-gather.4.cloned.1.call-start
  10.1 0.7 all-gather.4.cloned.1.call-update
  10.8 0.0 reduce-scatter.2.cloned.1.call-start
  11.5 0.7 reduce.1
  12.2 2.8 gather_fusion.1
  15.1 49.9 %all-gather.6.cloned.1.call-done = bf16[384,4096]{1,0:T(8,128)(2,1)} async-done(((bf16[384,256]{1,0:T(8,128)(2,1)}), bf16[384,4096]{1,0:T(8,128)(2,1)}) %all-gather.6.cloned.1.call-update) | async-done | bytes 3145744 | tf_op jit(solution)/shard_map/all_gather | solution.py:10
  65.0 154.0 %all-gather.4.cloned.1.call-done = bf16[3968,4096]{1,0:T(8,128)(2,1)} async-done(((bf16[496,4096]{1,0:T(8,128)(2,1)}), bf16[3968,4096]{1,0:T(8,128)(2,1)}) %all-gather.4.cloned.1.call-update) | async-done | bytes 32505872 | tf_op jit(solution)/shard_map/all_gather | solution.py:34
  219.0 21.9 %fusion.16 = (f32[384]{0:T(512)S(1)}, f32[384,3968]{1,0:T(8,128)}) fusion(bf16[384,4096]{1,0:T(8,128)(2,1)} %all-gather.6.cloned.1.call-done, bf16[3968,4096]{1,0:T(8,128)(2,1)} %all-gather.4.cloned.1.call-done), kind=kOutput, calls=%fused_computation.26 | convolution fusion | flops 12483772416 | bytes 41747968 | tf_op jit(solution)/shard_map/dot_general | solution.py:11
  240.8 33.2 %pmax.7 = f32[384]{0:T(512)S(1)} all-reduce(f32[384]{0:T(512)S(1)} %get-tuple-element.5), channel_id=1, replica_groups=mesh['dp'=8,'vocab'=16] {'vocab'}, use_global_device_ids=true, to_apply=%region_1.2 | all-reduce | flops 384 | bytes 3072 | tf_op jit(solution)/shard_map/pmax | solution.py:16
  274.1 3.7 fusion
  277.7 28.7 %psum.7 = f32[384]{0:T(512)S(1)} all-reduce(f32[384]{0:T(512)S(1)} %fusion), channel_id=1, replica_groups=mesh['dp'=8,'vocab'=16] {'vocab'}, use_global_device_ids=true, to_apply=%region_3.4 | all-reduce | flops 384 | bytes 3072 | tf_op jit(solution)/shard_map/psum | solution.py:17
  306.4 22.8 %convolution_convert_fusion = bf16[384,4096]{1,0:T(8,128)(2,1)} fusion(bf16[3968,4096]{1,0:T(8,128)(2,1)} %all-gather.4.cloned.1.call-done, f32[384,3968]{1,0:T(8,128)} %get-tuple-element.6, s32[3968]{0:T(1024)S(1)} %iota_add_fusion, f32[384]{0:T(512)S(1)} %psum.7, f32[384]{0:T(512)S(1)} %pmax.7, f32[384]{0:T(512)S(1)} %fusion.11, s32[384]{0:T(512)S(1)} %gather_fusion.1), kind=kOutput, calls=%fused_computation.5 | convolution fusion | flops 12496011264 | bytes 41768448 | tf_op jit(solution)/shard_map/dot_general | solution.py:23
  329.3 0.0 reduce-scatter.2.cloned.1.call-update
  329.3 85.4 %reduce-scatter.2.cloned.1.call-done = bf16[384,256]{1,0:T(8,128)(2,1)} async-done(((bf16[384,4096]{1,0:T(8,128)(2,1)}), bf16[384,256]{1,0:T(8,128)(2,1)}) %reduce-scatter.2.cloned.1.call-update) | async-done | bytes 196624 | tf_op jit(solution)/shard_map/reduce_scatter | solution.py:24
  414.7 2.9 scatter_custom_fusion
  (3 shorter events, 0.0 us)
Async XLA Ops:
  6.5 0.9 copy-start
  6.5 58.5 %all-gather.6.cloned.1.call-start = ((), (), s32[]{:S(2)}) async-start(), calls=%async_computation.3 | async-start | bytes 3342336 | tf_op jit(solution)/shard_map/all_gather | solution.py:10
  10.1 208.9 %all-gather.4.cloned.1.call-start = ((), (), s32[]{:S(2)}) async-start(), calls=%async_computation.1 | async-start | bytes 36569088 | tf_op jit(solution)/shard_map/all_gather | solution.py:34
  10.8 403.9 %reduce-scatter.2.cloned.1.call-start = ((), (), s32[]{:S(2)}) async-start(), calls=%async_computation.2 | async-start | bytes 3342336 | tf_op jit(solution)/shard_map/reduce_scatter | solution.py:24
Sparse Core Ops, SparseCore 0:
  10.2 54.7 all-gather.5
  66.7 152.2 all-gather.3
  329.4 85.2 reduce-scatter.1
where the time goes:
time: 425 us; the launch traced here: 424 us
  waiting for transfers between devices  290 us (68%)
  blocking collectives  61.9 us (15%)
  matrix products  44.7 us (11%)
  between operations  13.8 us (3%)
  local copies, waits for them, and re-layouts  8.45 us (2%)
  other arithmetic  5.14 us (1%)
    all_gather x1, waiting for transfers between devices, local(): group_weight = lax.all_gather(out_weight, 'dp', axis=0, tiled=True)  154 us
    reduce_scatter x1, waiting for transfers between devices, row_gradients(): lax.psum_scatter(partial_sum.astype(jnp.bfloat16), 'vocab', scatter_dimen...  85.4 us
    all_gather x1, waiting for transfers between devices, row_gradients(): whole = lax.all_gather(part_rows, 'vocab', axis=1, tiled=True)  49.9 us
    pmax x1, blocking collectives, row_gradients(): top_score = lax.pmax(jnp.max(scores, axis=1), 'vocab')  33.2 us
    psum x1, blocking collectives, row_gradients(): lax.psum(jnp.sum(jnp.exp(scores - top_score[:, None]), axis=1), 'vocab')  28.7 us
    dot_general x1, matrix products, row_gradients(): jnp.dot(dlogits, group_weight, preferred_element_type=jnp.float32)  22.8 us
    dot_general x1, matrix products, row_gradients(): lax.dot_general(whole, group_weight, (((1,), (1,)), ((), ())), preferred_...  21.9 us
  transfers between devices with their start and end apart: 3, of which 3 were waited for; matrix products, arithmetic and copies ran while one was open for 1% of the time, Pallas kernels for 0%

commit v1 on v0

v1 whole, which is shorter than its diff:
```python
import functools

import jax
import jax.numpy as jnp
from jax import lax
from jax.experimental import pallas as pl
from jax.experimental.pallas import tpu as pltpu
from jax.sharding import PartitionSpec as P

MESH = pl.DeviceIdType.MESH
F32, BF16 = jnp.float32, jnp.bfloat16
smoothing = 0.1

L = 384
DS = 256
RING = 4
D = DS * RING * RING
WR = 496
WC = 2 * WR
WP = 1024
VOCAB = WC * RING ** 3
ROWS = 768
CHUNKS = 2
CH = ROWS // CHUNKS
T = CH // 3
Q = T // RING
DEAD = 1.0e6
COPIES = 160


def kernel(hid, pos, tgt, cnt, w_in, out, x_buf, p_buf, w_buf, s_buf, d_buf, raw, meta, tcol, wcol, sel, st_buf, st_recv,
           ra1, ra2, rb1, rb2, rc1, rc2x, rc2y, rc3, sa, sb, sc, scx, scy, gab, rz, g_buf, w_sem, send_sem, recv_sem):
    dp, vocab = lax.axis_index("dp"), lax.axis_index("vocab")
    z, core = lax.div(dp, 2), lax.rem(dp, 2)
    x, y = lax.div(vocab, RING), lax.rem(vocab, RING)
    here = {"x": x, "y": y, "z": z}

    def step(axis, d):
        return lax.rem(here[axis] + d, RING)

    def device(axis, d):
        c = dict(here)
        k = core
        if axis == "core":
            k = 1 - core
        else:
            c[axis] = step(axis, d)
        return (c["z"] * 2 + k, c["x"] * RING + c["y"])

    used = [0]
    sent = []

    def remote(src, dst, axis, d):
        i = used[0]
        used[0] += 1
        copy = pltpu.make_async_remote_copy(
            src_ref=src, dst_ref=dst, send_sem=send_sem.at[i], recv_sem=recv_sem.at[i],
            device_id=device(axis, d), device_id_type=MESH,
        )
        copy.start()
        sent.append(copy)
        return copy

    def gather(axis, block):
        return [remote(block(here[axis]), block(here[axis]), axis, d) for d in (1, 3, 2)]

    def scatter(axis, block, landing):
        return [remote(block(step(axis, d)), landing.at[d - 1], axis, d) for d in (2, 1, 3)]

    def arrive(copies):
        for copy in copies:
            copy.wait_recv()

    def cols(i):
        return pl.ds(pl.multiple_of(i * DS, DS), DS)

    def quarter(i):
        return pl.ds(pl.multiple_of(i * Q, Q), Q)

    barrier = pltpu.get_barrier_semaphore()
    for axis in ("x", "y", "z"):
        for d in (1, 2, 3):
            pl.semaphore_signal(barrier, inc=1, device_id=device(axis, d), device_id_type=MESH)
    pl.semaphore_signal(barrier, inc=1, device_id=device("core", 0), device_id_type=MESH)

    own_rows = pl.ds(pl.multiple_of(core * WR, 16), WR)
    own_copy = pltpu.make_async_copy(w_in, w_buf.at[own_rows], w_sem)
    own_copy.start()

    raw[dp] = hid[...]
    count = jnp.full((1, L), cnt[0], jnp.int32).astype(F32)
    place = lax.broadcasted_iota(jnp.int32, (L, L), 0) == pos[...]
    entry = lax.broadcasted_iota(jnp.int32, (8, L), 1)
    half = lax.broadcasted_iota(jnp.int32, (8, L), 0)
    digits = jnp.where(half == 0, lax.div(entry, 128), lax.rem(entry, 128)).astype(F32).astype(BF16)
    found = lax.dot_general(digits, place.astype(F32).astype(BF16), (((1,), (1,)), ((), ())), preferred_element_type=F32)
    rank = found[0:1] * 128.0 + found[1:2]
    rank = jnp.where(rank < count, rank, DEAD)
    meta[dp, 0:1, :] = rank
    meta[dp, 1:2, :] = tgt[...].astype(F32)
    meta[dp, 2:3, :] = count
    meta[dp, 3:8, :] = jnp.zeros((5, L), F32)
    w_buf[WC:WP, :] = jnp.zeros((WP - WC, D), BF16)

    pl.semaphore_wait(barrier, 10)

    def slot(ref):
        return lambda i: ref.at[i * 2 + core]

    raw_z = gather("z", slot(raw))
    meta_z = gather("z", slot(meta))
    to_core = [remote(raw.at[dp], raw.at[dp], "core", 0), remote(meta.at[dp], meta.at[dp], "core", 0)]
    for n, d in enumerate((1, 3, 2)):
        source = step("z", 4 - d) * 2 + core
        raw_z[n].wait_recv()
        to_core.append(remote(raw.at[source], raw.at[source], "core", 0))
        meta_z[n].wait_recv()
        to_core.append(remote(meta.at[source], meta.at[source], "core", 0))
    w_copy = remote(w_in, w_buf.at[own_rows], "core", 0)
    arrive(to_core)

    counts = [meta[b, 2:3, :] for b in range(8)]
    starts = [jnp.zeros((1, L), F32)]
    for b in range(7):
        starts.append(starts[-1] + counts[b])

    def row_ids(first, rows, width):
        ids = lax.broadcasted_iota(jnp.int32, (rows, width), 0) + (core * ROWS + first)
        return ids.astype(F32)

    def compact_rows(first, rows):
        total = jnp.zeros((rows, DS), F32)
        ids = row_ids(first, rows, L)
        for b in range(8):
            match = ids == (starts[b] + meta[b, 0:1, :])
            total += jnp.dot(match.astype(F32).astype(BF16), raw[b], preferred_element_type=F32)
        return total.astype(BF16)

    def compact(chunk):
        r = chunk * CH
        for first in (r, r + T):
            x_buf[x, first:first + T, cols(y)] = compact_rows(first, T)
        first = r + 2 * T + z * Q
        x_buf[x, pl.ds(pl.multiple_of(first, Q), Q), cols(y)] = compact_rows(first, Q)

    def tables(chunk):
        for first in range(chunk * CH, chunk * CH + CH, 128):
            ids = row_ids(first, 128, L)
            target = jnp.zeros((128, L), F32)
            for b in range(8):
                match = ids == (starts[b] + meta[b, 0:1, :])
                target += jnp.where(match, meta[b, 1:2, :], 0.0)
            tcol[first:first + 128, :] = jnp.broadcast_to(jnp.sum(target, axis=1, keepdims=True), (128, 128))
            ids = row_ids(first, 128, 128)
            weight = jnp.zeros((128, 128), F32)
            for b in range(8):
                low, size = starts[b][:, :128], counts[b][:, :128]
                weight += jnp.where((ids >= low) & (ids < low + size), jnp.float32(L) / size, 0.0)
            wcol[first:first + 128, :] = weight

    def gather_1(chunk):
        r = chunk * CH
        a = gather("x", lambda i: x_buf.at[i, pl.ds(r, T), cols(y)])
        b = gather("y", lambda i: x_buf.at[x, pl.ds(r + T, T), cols(i)])
        rows = pl.ds(pl.multiple_of(r + 2 * T + z * Q, Q), Q)
        if chunk % 2 == 0:
            c = gather("x", lambda i: x_buf.at[i, rows, cols(y)])
        else:
            c = gather("y", lambda i: x_buf.at[x, rows, cols(i)])
        return a, b, c

    def gather_2(chunk, before):
        r = chunk * CH
        a, b, c = before
        rows = pl.ds(pl.multiple_of(r + 2 * T + z * Q, Q), Q)
        arrive(c)
        if chunk % 2 == 0:
            c = gather("y", lambda i: x_buf.at[:, rows, cols(i)])
        else:
            c = gather("x", lambda i: x_buf.at[i, rows, :])
        arrive(a)
        a = gather("y", lambda i: x_buf.at[:, pl.ds(r, T), cols(i)])
        arrive(b)
        b = gather("x", lambda i: x_buf.at[i, pl.ds(r + T, T), :])
        return a, b, c

    def gather_3(chunk, before):
        r = chunk * CH
        a, b, c = before
        arrive(c)
        c = gather("z", lambda i: x_buf.at[:, pl.ds(pl.multiple_of(r + 2 * T + i * Q, Q), Q), :])
        return a, b, c

    def scores(chunk):
        r = chunk * CH
        for n in range(0, WP, 256):
            total = jnp.zeros((CH, 256), F32)
            for i in range(RING):
                total += lax.dot_general(
                    x_buf[i, r:r + CH, :], w_buf[n:n + 256, i * 1024:(i + 1) * 1024], (((1,), (1,)), ((), ())),
                    preferred_element_type=F32,
                )
            s_buf[:, n:n + 256] = total

    lane = lax.broadcasted_iota(jnp.int32, (CH, 128), 1)

    def local_stats(chunk):
        tail = jnp.where(lane < WC - 7 * 128, s_buf[:, 7 * 128:8 * 128], -jnp.inf)
        s_buf[:, 7 * 128:8 * 128] = tail
        top = tail
        for t in range(7):
            top = jnp.maximum(top, s_buf[:, t * 128:(t + 1) * 128])
        top = jnp.max(top, axis=1, keepdims=True)
        total = jnp.zeros((CH, 128), F32)
        for t in range(8):
            e = jnp.exp(s_buf[:, t * 128:(t + 1) * 128] - top)
            s_buf[:, t * 128:(t + 1) * 128] = e
            total += e
        total = jnp.sum(total, axis=1, keepdims=True)
        both = jnp.where(lane == 0, top, total)
        st_buf[chunk, 0] = both.T[0:8]

    def send_stats(chunk, n, axis):
        return [remote(st_buf.at[chunk, n], st_recv.at[chunk, n, d - 1], axis, d) for d in (1, 3, 2)]

    def merge_stats(chunk, n, copies):
        arrive(copies)
        parts = [st_buf[chunk, n]] + [st_recv[chunk, n, d] for d in range(3)]
        top = parts[0][0:1]
        for part in parts[1:]:
            top = jnp.maximum(top, part[0:1])
        total = jnp.zeros((1, CH), F32)
        for part in parts:
            total += part[1:2] * jnp.exp(part[0:1] - top)
        rows = lax.broadcasted_iota(jnp.int32, (8, CH), 0)
        st_buf[chunk, n + 1] = jnp.where(rows == 0, top, total)

    def gradients(chunk):
        r = chunk * CH
        own, whole = st_buf[chunk, 0], st_buf[chunk, 3]
        scale = jnp.exp(own[0:1] - whole[0:1]) / whole[1:2]
        scale = jnp.broadcast_to(scale, (128, CH)).T
        weight = wcol[r:r + CH, :]
        target = tcol[r:r + CH, :]
        first = (vocab * 8 + z * 2) * WR
        for t in range(8):
            ids = (lane + (first + t * 128)).astype(F32)
            onehot = jnp.where(ids == target, 1.0 - smoothing, 0.0)
            probs = s_buf[:, t * 128:(t + 1) * 128] * scale
            d_buf[:, t * 128:(t + 1) * 128] = (weight * (probs - onehot - smoothing / VOCAB)).astype(BF16)

    def products(chunk):
        r = chunk * CH

        def body(n, carry):
            i, j = lax.div(n, RING), lax.rem(n, RING)
            p_buf[i, r:r + CH, cols(j)] = jnp.dot(
                d_buf[...], w_buf[:, cols(n)], preferred_element_type=F32
            ).astype(BF16)
            return carry

        lax.fori_loop(0, RING * RING, body, 0)

    def scatter_1(chunk):
        r = chunk * CH
        c = scatter("z", lambda i: p_buf.at[:, pl.ds(pl.multiple_of(r + 2 * T + i * Q, Q), Q), :], rc1.at[chunk])
        a = scatter("y", lambda i: p_buf.at[:, pl.ds(r, T), cols(i)], ra1.at[chunk])
        b = scatter("x", lambda i: p_buf.at[i, pl.ds(r + T, T), :], rb1.at[chunk])
        return a, b, c

    def added(own, landing):
        total = own.astype(F32)
        for d in range(3):
            total += landing[d].astype(F32)
        return total.astype(BF16)

    def scatter_2(chunk, before):
        r = chunk * CH
        a, b, c = before
        arrive(c)
        rows = pl.ds(pl.multiple_of(r + 2 * T + z * Q, Q), Q)
        for i in range(RING):
            sc[chunk, i] = added(p_buf[i, rows, :], [rc1[chunk, d, i] for d in range(3)])
        if chunk % 2 == 0:
            c = scatter("y", lambda i: sc.at[chunk, :, :, cols(i)], rc2y)
        else:
            c = scatter("x", lambda i: sc.at[chunk, i], rc2x)
        arrive(a)
        for i in range(RING):
            sa[chunk, i] = added(p_buf[i, r:r + T, cols(y)], [ra1[chunk, d, i] for d in range(3)])
        a = scatter("x", lambda i: sa.at[chunk, i], ra2.at[chunk])
        arrive(b)
        for h in range(0, T, 32):
            sb[chunk, h:h + 32, :] = added(
                p_buf[x, r + T + h:r + T + h + 32, :], [rb1[chunk, d, h:h + 32, :] for d in range(3)]
            )
        b = scatter("y", lambda i: sb.at[chunk, :, cols(i)], rb2.at[chunk])
        return a, b, c

    def scatter_3(chunk, before):
        a, b, c = before
        arrive(c)
        if chunk % 2 == 0:
            for i in range(RING):
                scy[i] = added(sc[chunk, i, :, cols(y)], [rc2y[d, i] for d in range(3)])
            c = scatter("x", lambda i: scy.at[i], rc3.at[chunk])
        else:
            scx[...] = added(sc[chunk, x], [rc2x[d] for d in range(3)])
            c = scatter("y", lambda i: scx.at[:, cols(i)], rc3.at[chunk])
        arrive(a)
        gab[chunk, 0] = added(sa[chunk, x], [ra2[chunk, d] for d in range(3)]).reshape(RING, Q, DS)
        arrive(b)
        gab[chunk, 1] = added(sb[chunk, :, cols(y)], [rb2[chunk, d] for d in range(3)]).reshape(RING, Q, DS)
        ab = scatter("z", lambda i: gab.at[chunk, :, i], rz.at[chunk])
        return ab, c

    def spread(chunk, before):
        ab, c = before
        arrive(c)
        own = scy[x] if chunk % 2 == 0 else scx[:, cols(y)]
        g_buf[core, chunk, 2, z] = added(own, [rc3[chunk, d] for d in range(3)])
        arrive(ab)
        for t in range(2):
            g_buf[core, chunk, t, z] = added(gab[chunk, t, z], [rz[chunk, d, t] for d in range(3)])
        block = lambda i: g_buf.at[core, chunk, :, i]
        copies = gather("z", block)
        over = [remote(block(z), block(z), "core", 0)]
        return copies, over

    def spread_over(chunk, before):
        copies, over = before
        block = lambda i: g_buf.at[core, chunk, :, i]
        for n, d in enumerate((1, 3, 2)):
            copies[n].wait_recv()
            over.append(remote(block(step("z", 4 - d)), block(step("z", 4 - d)), "core", 0))
        arrive(over)

    def selection():
        start = jnp.zeros((1, L), F32)
        for b in range(8):
            start += jnp.where(dp == b, starts[b], 0.0)
        where = start + rank
        where = jnp.broadcast_to(where, (128, L)).T
        for n in range(0, 2 * ROWS, 128):
            ids = lax.broadcasted_iota(jnp.int32, (L, 128), 1) + n
            sel[:, n:n + 128] = (where == ids.astype(F32)).astype(F32).astype(BF16)

    def place_rows(chunk, total):
        for k in range(2):
            first = k * ROWS + chunk * CH
            total += jnp.dot(
                sel[:, first:first + CH], g_buf[k, chunk].reshape(CH, DS), preferred_element_type=F32
            )
        return total

    compact(0)
    g0 = gather_1(0)
    compact(1)
    g1 = gather_1(1)
    g0 = gather_2(0, g0)
    tables(0)
    g0 = gather_3(0, g0)
    g1 = gather_2(1, g1)
    tables(1)
    selection()
    for group in g0:
        arrive(group)
    own_copy.wait()
    w_copy.wait_recv()
    scores(0)
    local_stats(0)
    s0 = send_stats(0, 0, "x")
    g1 = gather_3(1, g1)
    merge_stats(0, 0, s0)
    s0 = send_stats(0, 1, "y")
    merge_stats(0, 1, s0)
    s0 = send_stats(0, 2, "z")
    merge_stats(0, 2, s0)
    gradients(0)
    products(0)
    r0 = scatter_1(0)
    for group in g1:
        arrive(group)
    scores(1)
    local_stats(1)
    s1 = send_stats(1, 0, "x")
    r0 = scatter_2(0, r0)
    merge_stats(1, 0, s1)
    s1 = send_stats(1, 1, "y")
    merge_stats(1, 1, s1)
    s1 = send_stats(1, 2, "z")
    merge_stats(1, 2, s1)
    gradients(1)
    products(1)
    r1 = scatter_1(1)
    r0 = scatter_3(0, r0)
    r0 = spread(0, r0)
    r1 = scatter_2(1, r1)
    spread_over(0, r0)
    total = place_rows(0, jnp.zeros((L, DS), F32))
    r1 = scatter_3(1, r1)
    r1 = spread(1, r1)
    spread_over(1, r1)
    out[...] = place_rows(1, total).astype(BF16)
    for copy in sent:
        copy.wait_send()


def local(hidden, positions, targets, counts, out_weight):
    vmem = pl.BlockSpec(memory_space=pltpu.VMEM)
    return pl.pallas_call(
        kernel,
        out_shape=jax.ShapeDtypeStruct((L, DS), BF16),
        in_specs=[vmem, vmem, vmem, pl.BlockSpec(memory_space=pltpu.SMEM), pl.BlockSpec(memory_space=pl.ANY)],
        out_specs=vmem,
        scratch_shapes=[
            pltpu.VMEM((RING, ROWS, 1024), BF16),
            pltpu.VMEM((RING, ROWS, 1024), BF16),
            pltpu.VMEM((WP, D), BF16),
            pltpu.VMEM((CH, WP), F32),
            pltpu.VMEM((CH, WP), BF16),
            pltpu.VMEM((8, L, DS), BF16),
            pltpu.VMEM((8, 8, L), F32),
            pltpu.VMEM((ROWS, 128), F32),
            pltpu.VMEM((ROWS, 128), F32),
            pltpu.VMEM((L, 2 * ROWS), BF16),
            pltpu.VMEM((CHUNKS, 4, 8, CH), F32),
            pltpu.VMEM((CHUNKS, 3, 3, 8, CH), F32),
            pltpu.VMEM((CHUNKS, 3, RING, T, DS), BF16),
            pltpu.VMEM((CHUNKS, 3, T, DS), BF16),
            pltpu.VMEM((CHUNKS, 3, T, 1024), BF16),
            pltpu.VMEM((CHUNKS, 3, T, DS), BF16),
            pltpu.VMEM((CHUNKS, 3, RING, Q, 1024), BF16),
            pltpu.VMEM((3, Q, 1024), BF16),
            pltpu.VMEM((3, RING, Q, DS), BF16),
            pltpu.VMEM((CHUNKS, 3, Q, DS), BF16),
            pltpu.VMEM((CHUNKS, RING, T, DS), BF16),
            pltpu.VMEM((CHUNKS, T, 1024), BF16),
            pltpu.VMEM((CHUNKS, RING, Q, 1024), BF16),
            pltpu.VMEM((Q, 1024), BF16),
            pltpu.VMEM((RING, Q, DS), BF16),
            pltpu.VMEM((CHUNKS, 2, RING, Q, DS), BF16),
            pltpu.VMEM((CHUNKS, 3, 2, Q, DS), BF16),
            pltpu.VMEM((2, CHUNKS, 3, RING, Q, DS), BF16),
            pltpu.SemaphoreType.DMA,
            pltpu.SemaphoreType.DMA((COPIES,)),
            pltpu.SemaphoreType.DMA((COPIES,)),
        ],
        compiler_params=pltpu.CompilerParams(collective_id=0, has_side_effects=True, vmem_limit_bytes=56 << 20),
        cost_estimate=pl.CostEstimate(flops=4 * ROWS * WC * D, bytes_accessed=2 * WR * D, transcendentals=ROWS * WC),
        name="masked_row_gradient",
    )(hidden[0], positions, targets, counts, out_weight)[None]


def solution(mesh):
    return jax.shard_map(
        local,
        mesh=mesh,
        in_specs=(
            P("dp", None, "vocab"),
            P("dp", None),
            P("dp", None),
            P("dp"),
            P(("vocab", "dp"), None),
        ),
        out_specs=P("dp", None, "vocab"),
        check_vma=False,
    )
```

time: 425 us -> 142 us (0.33)
  waiting for transfers between devices: 290 us -> 0 us
  Pallas kernels: 0 us -> 139 us
  blocking collectives: 61.9 us -> 0 us
  matrix products: 44.7 us -> 0 us
  between operations: 13.8 us -> 0.66 us
  local copies, waits for them, and re-layouts: 8.45 us -> 1.62 us
  other arithmetic: 5.14 us -> 0 us
    all_gather x2 -> x0, waiting for transfers between devices: 204 us -> none  [the longest x1 154 us: local(): group_weight = lax.all_gather(out_weight, 'dp', axis=0, tiled=True)]
    pallas_call x0 -> x1, Pallas kernels: none -> 139 us  [local(): pl.pallas_call(kernel, out_shape=jax.ShapeDtypeStruct((L, DS), BF16), in_...]
    reduce_scatter x1 -> x0, waiting for transfers between devices: 85.4 us -> none  [row_gradients(): lax.psum_scatter(partial_sum.astype(jnp.bfloat16), 'vocab', scatter_dimen...]
    dot_general x2 -> x0, matrix products: 44.7 us -> none  [the longest x1 22.8 us: row_gradients(): jnp.dot(dlogits, group_weight, preferred_element_type=jnp.float32)]
    pmax x1 -> x0, blocking collectives: 33.2 us -> none  [row_gradients(): top_score = lax.pmax(jnp.max(scores, axis=1), 'vocab')]
    psum x1 -> x0, blocking collectives: 28.7 us -> none  [row_gradients(): lax.psum(jnp.sum(jnp.exp(scores - top_score[:, None]), axis=1), 'vocab')]
    gather x2 -> x0, local copies, waits for them, and re-layouts: 5.36 us -> none  [the longest x1 2.81 us: local(): row_targets = targets[0][place]]
  transfers between devices with their start and end apart: 3 -> 0, of which waited for: 3 -> 0; matrix products, arithmetic and copies ran while one was open for 1% -> 0% of each run, Pallas kernels for 0% -> 0%
where the time goes in v1:
time: 142 us; the launch traced here: 141 us
  Pallas kernels  139 us (98%)
  local copies, waits for them, and re-layouts  1.62 us (1%)
    pallas_call x1, Pallas kernels, local(): pl.pallas_call(kernel, out_shape=jax.ShapeDtypeStruct((L, DS), BF16), in_...  139 us

profile of v1, /device:TPU:1, one launch (start us, length us, event | category | flops | bytes accessed | tf_op | source)
XLA Modules:
  0.0 141.5 jit_solution(2529586514043343433)
XLA Ops:
  0.7 139.2 %masked_row_gradient.1 = bf16[384,256]{1,0:T(8,128)(2,1)} custom-call(bf16[384,256]{1,0:T(8,128)(2,1)} %bitcast.3, s32[1,384]{1,0:T(1,128)} %pos.1, s32[1,384]{1,0:T(1,128)} %tgt.1, s32[1]{0:T(128)S(6)} %copy.7.cnt, bf16[496,4096]{1,0:T(8,128)(2,1)} %w_in.1), custom_call_target="tpu_custom_call" | custom-call | flops 12482248704 | bytes 4063232 | tf_op jit(solution)/shard_map/masked_row_gradient/pallas_call | solution.py:411
  139.9 1.6 %copy.8 = bf16[1,384,256]{2,1,0:T(8,128)(2,1)} copy(bf16[1,384,256]{2,1,0:T(8,128)(2,1)} %bitcast.2) | data formatting | bytes 393216

commit v2 on v1

v2 whole, which is shorter than its diff:
```python
import jax
import jax.numpy as jnp
from jax import lax
from jax.experimental import pallas as pl
from jax.experimental.pallas import tpu as pltpu
from jax.sharding import PartitionSpec as P

MESH = pl.DeviceIdType.MESH
F32, BF16 = jnp.float32, jnp.bfloat16
smoothing = 0.1

L = 384
DS = 256
RING = 4
D = DS * RING * RING
DX = DS * RING
WR = 496
WC = 2 * WR
WP = 1024
VOCAB = WC * RING ** 3
ROWS = 768
CH = 256
CHUNKS = ROWS // CH
AROWS = (96, 64, 64)
CROWS = (64, 128, 128)
Y_FIRST = (True, True, False)
PART = CH // RING
DEAD = 1.0e6
COPIES = 320


def scratch():
    shapes = {
        "x": ((RING, ROWS, DX), BF16),
        "p": ((RING, ROWS, DX), BF16),
        "w": ((WP, D), BF16),
        "s": ((CHUNKS, CH, WP), F32),
        "d": ((CH, WP), BF16),
        "raw": ((8, L, DS), BF16),
        "meta": ((8, 8, L), F32),
        "target": ((ROWS, 128), F32),
        "weight": ((ROWS, 128), F32),
        "sel": ((L, 2 * ROWS), BF16),
        "st": ((CHUNKS, 4, 8, CH), F32),
        "st_in": ((CHUNKS, 3, 3, 8, CH), F32),
    }
    for k in range(CHUNKS):
        a, q = AROWS[k], CROWS[k] // RING
        shapes.update({
            f"a_far{k}": ((2, 2, a, DS), BF16),
            f"a_in{k}": ((2, RING, a, DS), BF16),
            f"b_far{k}": ((2, a // 2, DX), BF16),
            f"b_in{k}": ((2, a, DX), BF16),
            f"c_far{k}": ((2, 2, q, DX), BF16),
            f"c_in{k}": ((2, RING, q, DX), BF16),
            f"a_sum{k}": ((RING, a, DS), BF16),
            f"b_sum{k}": ((a, DX), BF16),
            f"c_sum{k}": ((RING, q, DX), BF16),
            f"a_in2{k}": ((3, a, DS), BF16),
            f"b_in2{k}": ((3, a, DS), BF16),
            f"c_in2{k}": ((3, q, DX) if Y_FIRST[k] else (3, RING, q, DS), BF16),
            f"c_sum2{k}": ((q, DX) if Y_FIRST[k] else (RING, q, DS), BF16),
            f"c_in3{k}": ((3, q, DS), BF16),
            f"ab{k}": ((2 * a, DS), BF16),
            f"ab_in{k}": ((3, a // 2, DS), BF16),
            f"g{k}": ((2, RING, PART, DS), BF16),
        })
    return shapes


def kernel(hid, pos, tgt, cnt, w_in, out, *refs):
    m = dict(zip(scratch(), refs))
    w_sem, send_sem, recv_sem = refs[len(m):]
    x_buf, p_buf, w_buf, s_buf, d_buf = m["x"], m["p"], m["w"], m["s"], m["d"]
    raw, meta, sel, st_buf, st_in = m["raw"], m["meta"], m["sel"], m["st"], m["st_in"]
    dp, vocab = lax.axis_index("dp"), lax.axis_index("vocab")
    z, core = lax.div(dp, 2), lax.rem(dp, 2)
    x, y = lax.div(vocab, RING), lax.rem(vocab, RING)
    here = {"x": x, "y": y, "z": z}

    def step(axis, d):
        return lax.rem(here[axis] + d, RING)

    def device(axis, d):
        c = dict(here)
        k = core
        if axis == "core":
            k = 1 - core
        else:
            c[axis] = step(axis, d)
        return (c["z"] * 2 + k, c["x"] * RING + c["y"])

    used = [0]
    sent = []

    def remote(src, dst, axis, d):
        i = used[0]
        used[0] += 1
        copy = pltpu.make_async_remote_copy(
            src_ref=src, dst_ref=dst, send_sem=send_sem.at[i], recv_sem=recv_sem.at[i],
            device_id=device(axis, d), device_id_type=MESH,
        )
        copy.start()
        sent.append(copy)
        return copy

    def gather(axis, block):
        return [remote(block(here[axis]), block(here[axis]), axis, d) for d in (1, 3, 2)]

    def scatter(axis, block, landing):
        return [remote(block(step(axis, d)), landing.at[d - 1], axis, d) for d in (2, 1, 3)]

    def arrive(copies):
        for copy in copies:
            copy.wait_recv()

    def cols(i):
        return pl.ds(pl.multiple_of(i * DS, DS), DS)

    barrier = pltpu.get_barrier_semaphore()
    for axis in ("x", "y", "z"):
        for d in (1, 2, 3):
            pl.semaphore_signal(barrier, inc=1, device_id=device(axis, d), device_id_type=MESH)
    pl.semaphore_signal(barrier, inc=1, device_id=device("core", 0), device_id_type=MESH)

    own_rows = pl.ds(pl.multiple_of(core * WR, 16), WR)
    own_copy = pltpu.make_async_copy(w_in, w_buf.at[own_rows], w_sem)
    own_copy.start()

    raw[dp] = hid[...]
    count = jnp.full((1, L), cnt[0], jnp.int32).astype(F32)
    place = lax.broadcasted_iota(jnp.int32, (L, L), 0) == pos[...]
    entry = lax.broadcasted_iota(jnp.int32, (8, L), 1)
    half = lax.broadcasted_iota(jnp.int32, (8, L), 0)
    digits = jnp.where(half == 0, lax.div(entry, 128), lax.rem(entry, 128)).astype(F32).astype(BF16)
    found = lax.dot_general(digits, place.astype(F32).astype(BF16), (((1,), (1,)), ((), ())), preferred_element_type=F32)
    rank = found[0:1] * 128.0 + found[1:2]
    rank = jnp.where(rank < count, rank, DEAD)
    meta[dp, 0:1, :] = rank
    meta[dp, 1:2, :] = tgt[...].astype(F32)
    meta[dp, 2:3, :] = count
    meta[dp, 3:8, :] = jnp.zeros((5, L), F32)
    w_buf[WC:WP, :] = jnp.zeros((WP - WC, D), BF16)

    pl.semaphore_wait(barrier, 10)

    def slot(ref):
        return lambda i: ref.at[i * 2 + core]

    raw_z = gather("z", slot(raw))
    meta_z = gather("z", slot(meta))
    to_core = [remote(raw.at[dp], raw.at[dp], "core", 0), remote(meta.at[dp], meta.at[dp], "core", 0)]
    for n, d in enumerate((1, 3, 2)):
        source = step("z", 4 - d) * 2 + core
        raw_z[n].wait_recv()
        to_core.append(remote(raw.at[source], raw.at[source], "core", 0))
        meta_z[n].wait_recv()
        to_core.append(remote(meta.at[source], meta.at[source], "core", 0))
    w_copy = remote(w_in, w_buf.at[own_rows], "core", 0)
    arrive(to_core)

    counts = [meta[b, 2:3, :] for b in range(8)]
    starts = [jnp.zeros((1, L), F32)]
    for b in range(7):
        starts.append(starts[-1] + counts[b])

    def row_ids(first, rows, width):
        ids = lax.broadcasted_iota(jnp.int32, (rows, width), 0) + (core * ROWS + first)
        return ids.astype(F32)

    def near_1(axis, half):
        me = here[axis]
        return [remote(half(me, h), half(me, h), axis, d) for h, d in ((0, 1), (1, 3), (1, 1), (0, 3))]

    def near_2(axis, half, before):
        left, right = step(axis, 3), step(axis, 1)
        before[0].wait_recv()
        far_0 = remote(half(left, 0), half(left, 0), axis, 1)
        before[1].wait_recv()
        far_1 = remote(half(right, 1), half(right, 1), axis, 3)
        return [before[2], before[3], far_0, far_1]

    def sums_1(axis, half, far, landing):
        opposite, left, right = step(axis, 2), step(axis, 3), step(axis, 1)
        return [
            remote(half(opposite, 0), far.at[0], axis, 1),
            remote(half(opposite, 1), far.at[1], axis, 3),
            remote(half(right, 1), landing(0, 1), axis, 1),
            remote(half(left, 0), landing(1, 0), axis, 3),
        ]

    def sums_2(axis, half, far, landing, before):
        left, right = step(axis, 3), step(axis, 1)
        copies = before[2:]
        for n, (block, h, d) in enumerate(((right, 0, 1), (left, 1, 3))):
            before[n].wait_recv()
            ref = half(block, h)
            ref[...] = added(ref[...], [far[n]])
            copies.append(remote(ref, landing(n, h), axis, d))
        return copies

    def added(own, others):
        total = own.astype(F32)
        for other in others:
            total += other.astype(F32)
        return total.astype(BF16)

    def a_rows(k):
        return pl.ds(k * CH, AROWS[k])

    def b_rows(k):
        return pl.ds(k * CH + AROWS[k], AROWS[k])

    def c_rows(k, i):
        q = CROWS[k] // RING
        return pl.ds(pl.multiple_of(k * CH + 2 * AROWS[k] + i * q, 16), q)

    def a_half(ref, k):
        return lambda i, h: ref.at[2 * h:2 * h + 2, a_rows(k), cols(i)]

    def b_half(ref, k):
        a = AROWS[k]
        return lambda i, h: ref.at[i, pl.ds(k * CH + a + h * (a // 2), a // 2), :]

    def c_half(ref, k):
        return lambda i, h: ref.at[2 * h:2 * h + 2, c_rows(k, i), :]

    def a_land(k):
        return lambda n, h: m[f"a_in{k}"].at[n, 2 * h:2 * h + 2]

    def b_land(k):
        a = AROWS[k]
        return lambda n, h: m[f"b_in{k}"].at[n, h * (a // 2):(h + 1) * (a // 2), :]

    def c_land(k):
        return lambda n, h: m[f"c_in{k}"].at[n, 2 * h:2 * h + 2]

    def compact_rows(first, rows):
        total = jnp.zeros((rows, DS), F32)
        ids = row_ids(first, rows, L)
        for b in range(8):
            match = ids == (starts[b] + meta[b, 0:1, :])
            total += jnp.dot(match.astype(F32).astype(BF16), raw[b], preferred_element_type=F32)
        return total.astype(BF16)

    def compact_c(k):
        q = CROWS[k] // RING
        x_buf[x, c_rows(k, z), cols(y)] = compact_rows(k * CH + 2 * AROWS[k] + z * q, q)
        if Y_FIRST[k]:
            return gather("y", lambda i: x_buf.at[x, c_rows(k, z), cols(i)])
        return gather("x", lambda i: x_buf.at[i, c_rows(k, z), cols(y)])

    def gather_c(k, before):
        arrive(before)
        if Y_FIRST[k]:
            return gather("x", lambda i: x_buf.at[i, c_rows(k, z), :])
        return gather("y", lambda i: x_buf.at[:, c_rows(k, z), cols(i)])

    def compact_ab(k):
        a = AROWS[k]
        x_buf[x, k * CH:k * CH + 2 * a, cols(y)] = compact_rows(k * CH, 2 * a)
        return (gather("x", lambda i: x_buf.at[i, a_rows(k), cols(y)]),
                gather("y", lambda i: x_buf.at[x, b_rows(k), cols(i)]))

    def gather_ab(k, before):
        arrive(before[0])
        a = near_1("y", a_half(x_buf, k))
        arrive(before[1])
        b = near_1("x", b_half(x_buf, k))
        return a, b

    def hand_on_ab(k, before):
        return (near_2("y", a_half(x_buf, k), before[0]) + near_2("x", b_half(x_buf, k), before[1]))

    def gather_z(k, before):
        arrive(before)
        return near_1("z", c_half(x_buf, k))

    def hand_on_z(k, before):
        return near_2("z", c_half(x_buf, k), before)

    def tables(k):
        for first in range(k * CH, k * CH + CH, 128):
            ids = row_ids(first, 128, L)
            target = jnp.zeros((128, L), F32)
            for b in range(8):
                match = ids == (starts[b] + meta[b, 0:1, :])
                target += jnp.where(match, meta[b, 1:2, :], 0.0)
            m["target"][first:first + 128, :] = jnp.broadcast_to(jnp.sum(target, axis=1, keepdims=True), (128, 128))
            ids = row_ids(first, 128, 128)
            weight = jnp.zeros((128, 128), F32)
            for b in range(8):
                low, size = starts[b][:, :128], counts[b][:, :128]
                weight += jnp.where((ids >= low) & (ids < low + size), jnp.float32(L) / size, 0.0)
            m["weight"][first:first + 128, :] = weight

    lane = lax.broadcasted_iota(jnp.int32, (CH, 128), 1)

    def scores(k):
        r = k * CH
        for n in range(0, WP, 256):
            total = jnp.zeros((CH, 256), F32)
            for i in range(RING):
                total += lax.dot_general(
                    x_buf[i, r:r + CH, :], w_buf[n:n + 256, i * DX:(i + 1) * DX], (((1,), (1,)), ((), ())),
                    preferred_element_type=F32,
                )
            s_buf[k, :, n:n + 256] = total
        tail = jnp.where(lane < WC - 7 * 128, s_buf[k, :, 7 * 128:8 * 128], -jnp.inf)
        s_buf[k, :, 7 * 128:8 * 128] = tail
        top = tail
        for t in range(7):
            top = jnp.maximum(top, s_buf[k, :, t * 128:(t + 1) * 128])
        top = jnp.max(top, axis=1, keepdims=True)
        total = jnp.zeros((CH, 128), F32)
        for t in range(8):
            e = jnp.exp(s_buf[k, :, t * 128:(t + 1) * 128] - top)
            s_buf[k, :, t * 128:(t + 1) * 128] = e
            total += e
        total = jnp.sum(total, axis=1, keepdims=True)
        both = jnp.where(lane == 0, top, total)
        st_buf[k, 0] = both.T[0:8]

    axes = ("x", "y", "z")

    def send_stats(k, n):
        return [remote(st_buf.at[k, n], st_in.at[k, n, d - 1], axes[n], d) for d in (1, 3, 2)]

    def merge_stats(k, n, copies):
        arrive(copies)
        parts = [st_buf[k, n]] + [st_in[k, n, d] for d in range(3)]
        top = parts[0][0:1]
        for part in parts[1:]:
            top = jnp.maximum(top, part[0:1])
        total = jnp.zeros((1, CH), F32)
        for part in parts:
            total += part[1:2] * jnp.exp(part[0:1] - top)
        rows = lax.broadcasted_iota(jnp.int32, (8, CH), 0)
        st_buf[k, n + 1] = jnp.where(rows == 0, top, total)
        return send_stats(k, n + 1) if n < 2 else None

    def products(k):
        r = k * CH
        own, whole = st_buf[k, 0], st_buf[k, 3]
        scale = jnp.exp(own[0:1] - whole[0:1]) / whole[1:2]
        scale = jnp.broadcast_to(scale, (128, CH)).T
        weight = m["weight"][r:r + CH, :]
        target = m["target"][r:r + CH, :]
        first = (vocab * 8 + z * 2) * WR
        for t in range(8):
            ids = (lane + (first + t * 128)).astype(F32)
            onehot = jnp.where(ids == target, 1.0 - smoothing, 0.0)
            probs = s_buf[k, :, t * 128:(t + 1) * 128] * scale
            d_buf[:, t * 128:(t + 1) * 128] = (weight * (probs - onehot - smoothing / VOCAB)).astype(BF16)

        def body(i, carry):
            for j in range(RING):
                p_buf[i, r:r + CH, j * DS:(j + 1) * DS] = jnp.dot(
                    d_buf[...], w_buf[:, cols(i * RING + j)], preferred_element_type=F32
                ).astype(BF16)
            return carry

        lax.fori_loop(0, RING, body, 0)

    def scatter_1(k):
        return (sums_1("z", c_half(p_buf, k), m[f"c_far{k}"], c_land(k)),
                sums_1("y", a_half(p_buf, k), m[f"a_far{k}"], a_land(k)),
                sums_1("x", b_half(p_buf, k), m[f"b_far{k}"], b_land(k)))

    def scatter_2(k, before):
        return (sums_2("z", c_half(p_buf, k), m[f"c_far{k}"], c_land(k), before[0]),
                sums_2("y", a_half(p_buf, k), m[f"a_far{k}"], a_land(k), before[1]),
                sums_2("x", b_half(p_buf, k), m[f"b_far{k}"], b_land(k), before[2]))

    def scatter_3(k, before):
        arrive(before[0])
        c_sum, c_in = m[f"c_sum{k}"], m[f"c_in{k}"]
        for i in range(RING):
            c_sum[i] = added(p_buf[i, c_rows(k, z), :], [c_in[0, i], c_in[1, i]])
        if Y_FIRST[k]:
            c = scatter("x", lambda i: c_sum.at[i], m[f"c_in2{k}"])
        else:
            c = scatter("y", lambda i: c_sum.at[:, :, cols(i)], m[f"c_in2{k}"])
        arrive(before[1])
        a_sum, a_in = m[f"a_sum{k}"], m[f"a_in{k}"]
        for i in range(RING):
            a_sum[i] = added(p_buf[i, a_rows(k), cols(y)], [a_in[0, i], a_in[1, i]])
        a = scatter("x", lambda i: a_sum.at[i], m[f"a_in2{k}"])
        arrive(before[2])
        b_sum, b_in = m[f"b_sum{k}"], m[f"b_in{k}"]
        for h in range(0, AROWS[k], 32):
            own = p_buf[x, k * CH + AROWS[k] + h:k * CH + AROWS[k] + h + 32, :]
            b_sum[h:h + 32, :] = added(own, [b_in[0, h:h + 32, :], b_in[1, h:h + 32, :]])
        b = scatter("y", lambda i: b_sum.at[:, cols(i)], m[f"b_in2{k}"])
        return a, b, c

    def scatter_4(k, before):
        a, b, c = before
        n = AROWS[k]
        c_sum, c_in2, c_sum2 = m[f"c_sum{k}"], m[f"c_in2{k}"], m[f"c_sum2{k}"]
        arrive(c)
        if Y_FIRST[k]:
            c_sum2[...] = added(c_sum[x], [c_in2[d] for d in range(3)])
            c = scatter("y", lambda i: c_sum2.at[:, cols(i)], m[f"c_in3{k}"])
        else:
            for i in range(RING):
                c_sum2[i] = added(c_sum[i, :, cols(y)], [c_in2[d, i] for d in range(3)])
            c = scatter("x", lambda i: c_sum2.at[i], m[f"c_in3{k}"])
        ab = m[f"ab{k}"]
        arrive(a)
        ab[0:n, :] = added(m[f"a_sum{k}"][x], [m[f"a_in2{k}"][d] for d in range(3)])
        arrive(b)
        ab[n:2 * n, :] = added(m[f"b_sum{k}"][:, cols(y)], [m[f"b_in2{k}"][d] for d in range(3)])
        ab = scatter("z", lambda i: ab.at[pl.ds(pl.multiple_of(i * (n // 2), 16), n // 2), :], m[f"ab_in{k}"])
        return ab, c

    def spread(k, before):
        ab, c = before
        n = AROWS[k] // 2
        g, c_sum2 = m[f"g{k}"], m[f"c_sum2{k}"]
        arrive(c)
        own = c_sum2[:, cols(y)] if Y_FIRST[k] else c_sum2[x]
        g[core, z, n:PART, :] = added(own, [m[f"c_in3{k}"][d] for d in range(3)])
        arrive(ab)
        own = m[f"ab{k}"][pl.ds(pl.multiple_of(z * n, 16), n), :]
        g[core, z, 0:n, :] = added(own, [m[f"ab_in{k}"][d] for d in range(3)])
        copies = gather("z", lambda i: g.at[core, i])
        return copies, [remote(g.at[core, z], g.at[core, z], "core", 0)]

    def spread_over(k, before):
        copies, over = before
        g = m[f"g{k}"]
        for n, d in enumerate((1, 3, 2)):
            copies[n].wait_recv()
            block = g.at[core, step("z", 4 - d)]
            over.append(remote(block, block, "core", 0))
        arrive(over)

    def selection():
        start = jnp.zeros((1, L), F32)
        for b in range(8):
            start += jnp.where(dp == b, starts[b], 0.0)
        where = start + rank
        where = jnp.broadcast_to(where, (128, L)).T
        ids = lax.broadcasted_iota(jnp.int32, (L, 128), 1)
        for side in range(2):
            for k in range(CHUNKS):
                n, q = AROWS[k] // 2, CROWS[k] // RING
                for t in range(2):
                    i = ids & (PART - 1)
                    zi = (ids >> 6) + 2 * t
                    rows = jnp.where(i < n, zi * n + i, 4 * n + zi * q + i - n) + (side * ROWS + k * CH)
                    first = side * ROWS + k * CH + t * 128
                    sel[:, first:first + 128] = (where == rows.astype(F32)).astype(F32).astype(BF16)

    def place_rows(k, total):
        for side in range(2):
            first = side * ROWS + k * CH
            total += jnp.dot(
                sel[:, first:first + CH], m[f"g{k}"][side].reshape(CH, DS), preferred_element_type=F32
            )
        return total

    c0 = compact_c(0)
    ab0 = compact_ab(0)
    c1 = compact_c(1)
    ab1 = compact_ab(1)
    c0 = gather_c(0, c0)
    ab0 = gather_ab(0, ab0)
    c2 = compact_c(2)
    ab2 = compact_ab(2)
    c0 = gather_z(0, c0)
    c1 = gather_c(1, c1)
    ab0 = hand_on_ab(0, ab0)
    ab1 = gather_ab(1, ab1)
    c0 = hand_on_z(0, c0)
    c1 = gather_z(1, c1)
    c2 = gather_c(2, c2)
    tables(0)
    arrive(ab0 + c0)
    own_copy.wait()
    w_copy.wait_recv()
    scores(0)
    s0 = send_stats(0, 0)
    ab1 = hand_on_ab(1, ab1)
    c1 = hand_on_z(1, c1)
    ab2 = gather_ab(2, ab2)
    c2 = gather_z(2, c2)
    tables(1)
    s0 = merge_stats(0, 0, s0)
    arrive(ab1 + c1)
    scores(1)
    s1 = send_stats(1, 0)
    s0 = merge_stats(0, 1, s0)
    ab2 = hand_on_ab(2, ab2)
    c2 = hand_on_z(2, c2)
    merge_stats(0, 2, s0)
    products(0)
    r0 = scatter_1(0)
    s1 = merge_stats(1, 0, s1)
    tables(2)
    selection()
    arrive(ab2 + c2)
    scores(2)
    s2 = send_stats(2, 0)
    s1 = merge_stats(1, 1, s1)
    r0 = scatter_2(0, r0)
    merge_stats(1, 2, s1)
    products(1)
    s2 = merge_stats(2, 0, s2)
    r1 = scatter_1(1)
    s2 = merge_stats(2, 1, s2)
    r0 = scatter_3(0, r0)
    merge_stats(2, 2, s2)
    products(2)
    r1 = scatter_2(1, r1)
    r2 = scatter_1(2)
    r0 = scatter_4(0, r0)
    r1 = scatter_3(1, r1)
    r2 = scatter_2(2, r2)
    r0 = spread(0, r0)
    r1 = scatter_4(1, r1)
    spread_over(0, r0)
    r2 = scatter_3(2, r2)
    r1 = spread(1, r1)
    total = place_rows(0, jnp.zeros((L, DS), F32))
    r2 = scatter_4(2, r2)
    spread_over(1, r1)
    total = place_rows(1, total)
    r2 = spread(2, r2)
    spread_over(2, r2)
    out[...] = place_rows(2, total).astype(BF16)
    for copy in sent:
        copy.wait_send()


def local(hidden, positions, targets, counts, out_weight):
    vmem = pl.BlockSpec(memory_space=pltpu.VMEM)
    return pl.pallas_call(
        kernel,
        out_shape=jax.ShapeDtypeStruct((L, DS), BF16),
        in_specs=[vmem, vmem, vmem, pl.BlockSpec(memory_space=pltpu.SMEM), pl.BlockSpec(memory_space=pl.ANY)],
        out_specs=vmem,
        scratch_shapes=[
            *(pltpu.VMEM(shape, dtype) for shape, dtype in scratch().values()),
            pltpu.SemaphoreType.DMA,
            pltpu.SemaphoreType.DMA((COPIES,)),
            pltpu.SemaphoreType.DMA((COPIES,)),
        ],
        compiler_params=pltpu.CompilerParams(collective_id=0, has_side_effects=True, vmem_limit_bytes=56 << 20),
        cost_estimate=pl.CostEstimate(flops=4 * ROWS * WC * D, bytes_accessed=2 * WR * D, transcendentals=ROWS * WC),
        name="masked_row_gradient",
    )(hidden[0], positions, targets, counts, out_weight)[None]


def solution(mesh):
    return jax.shard_map(
        local,
        mesh=mesh,
        in_specs=(
            P("dp", None, "vocab"),
            P("dp", None),
            P("dp", None),
            P("dp"),
            P(("vocab", "dp"), None),
        ),
        out_specs=P("dp", None, "vocab"),
        check_vma=False,
    )
```

time: 142 us -> 124 us (0.87)
  Pallas kernels: 139 us -> 122 us
    pallas_call x1, Pallas kernels: 139 us -> 122 us  [local(): pl.pallas_call(kernel, out_shape=jax.ShapeDtypeStruct((L, DS), BF16), in_...]
where the time goes in v2:
time: 124 us
  Pallas kernels  122 us (98%)
  local copies, waits for them, and re-layouts  1.62 us (1%)
    pallas_call x1, Pallas kernels, local(): pl.pallas_call(kernel, out_shape=jax.ShapeDtypeStruct((L, DS), BF16), in_...  122 us

profile of v2, /device:TPU:1, one launch (start us, length us, event | category | flops | bytes accessed | tf_op | source)
XLA Modules:
  0.0 124.2 jit_solution(5955494232597154289)
XLA Ops:
  0.7 121.9 %masked_row_gradient.1 = bf16[384,256]{1,0:T(8,128)(2,1)} custom-call(bf16[384,256]{1,0:T(8,128)(2,1)} %bitcast.3, s32[1,384]{1,0:T(1,128)} %pos.1, s32[1,384]{1,0:T(1,128)} %tgt.1, s32[1]{0:T(128)S(6)} %copy.7.cnt, bf16[496,4096]{1,0:T(8,128)(2,1)} %w_in.1), custom_call_target="tpu_custom_call" | custom-call | flops 12482248704 | bytes 4063232 | tf_op jit(solution)/shard_map/masked_row_gradient/pallas_call | solution.py:539
  122.6 1.6 %copy.8 = bf16[1,384,256]{2,1,0:T(8,128)(2,1)} copy(bf16[1,384,256]{2,1,0:T(8,128)(2,1)} %bitcast.2) | data formatting | bytes 393216

commit v3 on v2

v3 whole, which is shorter than its diff:
```python
import jax
import jax.numpy as jnp
from jax import lax
from jax.experimental import pallas as pl
from jax.experimental.pallas import tpu as pltpu
from jax.sharding import PartitionSpec as P

MESH = pl.DeviceIdType.MESH
F32, BF16 = jnp.float32, jnp.bfloat16
smoothing = 0.1

L = 384
DS = 256
RING = 4
D = DS * RING * RING
DX = DS * RING
WR = 496
WC = 2 * WR
WP = 1024
VOCAB = WC * RING ** 3
ROWS = 768
CH = 256
CHUNKS = ROWS // CH
AROWS = (96, 64, 96)
CROWS = (64, 128, 64)
Y_FIRST = (True, False, True)
PART = CH // RING
DEAD = 1.0e6
ARRIVALS = 128
SENDS = 32
UNIT = 16 * DS * 2
UNITS = 128


def scratch():
    shapes = {
        "x": ((RING, ROWS, DX), BF16),
        "p": ((RING, ROWS, DX), BF16),
        "w": ((WP, D), BF16),
        "s": ((CHUNKS, CH, WP), F32),
        "d": ((CH, WP), BF16),
        "raw": ((8, L, DS), BF16),
        "unit": ((UNITS, 16, DS), BF16),
        "meta": ((8, 8, 512), F32),
        "target": ((ROWS, 128), F32),
        "weight": ((ROWS, 128), F32),
        "sel": ((L, 2 * ROWS), BF16),
        "st": ((CHUNKS, 4, 8, CH), F32),
        "st_in": ((CHUNKS, 3, 3, 8, CH), F32),
    }
    for k in range(CHUNKS):
        a, q = AROWS[k], CROWS[k] // RING
        shapes.update({
            ("a_far", k): ((2, 2, a, DS), BF16),
            ("a_in", k): ((2, RING, a, DS), BF16),
            ("b_far", k): ((2, a // 2, DX), BF16),
            ("b_in", k): ((2, a, DX), BF16),
            ("c_far", k): ((2, 2, q, DX), BF16),
            ("c_in", k): ((2, RING, q, DX), BF16),
            ("a_sum", k): ((RING, a, DS), BF16),
            ("b_sum", k): ((a, DX), BF16),
            ("c_sum", k): ((RING, q, DX), BF16),
            ("a_in2", k): ((3, a, DS), BF16),
            ("b_in2", k): ((3, a, DS), BF16),
            ("c_in2", k): ((3, q, DX) if Y_FIRST[k] else (3, RING, q, DS), BF16),
            ("c_sum2", k): ((q, DX) if Y_FIRST[k] else (RING, q, DS), BF16),
            ("c_in3", k): ((3, q, DS), BF16),
            ("ab", k): ((2 * a, DS), BF16),
            ("ab_in", k): ((3, a // 2, DS), BF16),
            ("g", k): ((2, RING, PART, DS), BF16),
        })
    return shapes


def kernel(hid, pos, tgt, cnt, w_in, out, *refs):
    m = dict(zip(scratch(), refs))
    w_sem, send_sem, recv_sem = refs[len(m):]
    x_buf, p_buf, w_buf, s_buf, d_buf = m["x"], m["p"], m["w"], m["s"], m["d"]
    raw, meta, sel, st_buf, st_in = m["raw"], m["meta"], m["sel"], m["st"], m["st_in"]
    dp, vocab = lax.axis_index("dp"), lax.axis_index("vocab")
    z, core = lax.div(dp, 2), lax.rem(dp, 2)
    x, y = lax.div(vocab, RING), lax.rem(vocab, RING)
    here = {"x": x, "y": y, "z": z}

    def step(axis, d):
        return lax.rem(here[axis] + d, RING)

    def device(axis, d):
        c = dict(here)
        k = core
        if axis == "core":
            k = 1 - core
        else:
            c[axis] = step(axis, d)
        return (c["z"] * 2 + k, c["x"] * RING + c["y"])

    arrivals = [0]
    sends = [[0, 0]]

    def weigh(ref):
        size = 2 if ref.dtype == BF16 else 4
        for n in ref.shape:
            size *= n
        assert size % UNIT == 0
        return size // UNIT

    def settle(semaphore, units):
        whole = m["unit"].at[0:units]
        pltpu.make_async_copy(whole, whole, semaphore).wait()

    def group():
        arrivals[0] += 1
        return [arrivals[0] - 1, 0]

    def remote(src, dst, axis, d, to):
        units = weigh(src)
        if sends[-1][1] + units > UNITS:
            sends.append([len(sends), 0])
        sends[-1][1] += units
        to[1] += units
        pltpu.make_async_remote_copy(
            src_ref=src, dst_ref=dst, send_sem=send_sem.at[sends[-1][0]], recv_sem=recv_sem.at[to[0]],
            device_id=device(axis, d), device_id_type=MESH,
        ).start()

    def gather(axis, block):
        to = group()
        for d in (1, 3, 2):
            remote(block(here[axis]), block(here[axis]), axis, d, to)
        return to

    def scatter(axis, block, landing):
        to = group()
        for d in (2, 1, 3):
            remote(block(step(axis, d)), landing.at[d - 1], axis, d, to)
        return to

    def arrive(to):
        settle(recv_sem.at[to[0]], to[1])

    def cols(i):
        return pl.ds(pl.multiple_of(i * DS, DS), DS)

    barrier = pltpu.get_barrier_semaphore()
    for axis in ("x", "y", "z"):
        for d in (1, 2, 3):
            pl.semaphore_signal(barrier, inc=1, device_id=device(axis, d), device_id_type=MESH)
    pl.semaphore_signal(barrier, inc=1, device_id=device("core", 0), device_id_type=MESH)

    own_rows = pl.ds(pl.multiple_of(core * WR, 16), WR)
    own_copy = pltpu.make_async_copy(w_in, w_buf.at[own_rows], w_sem.at[0])
    own_copy.start()

    raw[dp] = hid[...]
    count = jnp.full((1, L), cnt[0], jnp.int32).astype(F32)
    place = lax.broadcasted_iota(jnp.int32, (L, L), 0) == pos[...]
    entry = lax.broadcasted_iota(jnp.int32, (8, L), 1)
    half = lax.broadcasted_iota(jnp.int32, (8, L), 0)
    digits = jnp.where(half == 0, lax.div(entry, 128), lax.rem(entry, 128)).astype(F32).astype(BF16)
    found = lax.dot_general(digits, place.astype(F32).astype(BF16), (((1,), (1,)), ((), ())), preferred_element_type=F32)
    rank = found[0:1] * 128.0 + found[1:2]
    rank = jnp.where(rank < count, rank, DEAD)
    meta[dp] = jnp.zeros((8, 512), F32)
    meta[dp, 0:1, 0:L] = rank
    meta[dp, 1:2, 0:L] = tgt[...].astype(F32)
    meta[dp, 2:3, 0:L] = count
    w_buf[WC:WP, :] = jnp.zeros((WP - WC, D), BF16)

    pl.semaphore_wait(barrier, 10)

    near = [group() for _ in range(3)]
    other = group()
    for n, d in enumerate((1, 3, 2)):
        remote(raw.at[dp], raw.at[dp], "z", d, near[n])
        remote(meta.at[dp], meta.at[dp], "z", d, near[n])
    remote(raw.at[dp], raw.at[dp], "core", 0, other)
    remote(meta.at[dp], meta.at[dp], "core", 0, other)
    for n, d in enumerate((1, 3, 2)):
        source = step("z", 4 - d) * 2 + core
        arrive(near[n])
        remote(raw.at[source], raw.at[source], "core", 0, other)
        remote(meta.at[source], meta.at[source], "core", 0, other)
    w_copy = pltpu.make_async_remote_copy(
        src_ref=w_in, dst_ref=w_buf.at[own_rows], send_sem=w_sem.at[1], recv_sem=w_sem.at[2],
        device_id=device("core", 0), device_id_type=MESH,
    )
    w_copy.start()
    arrive(other)

    counts = [meta[b, 2:3, 0:L] for b in range(8)]
    starts = [jnp.zeros((1, L), F32)]
    for b in range(7):
        starts.append(starts[-1] + counts[b])

    def row_ids(first, rows, width):
        ids = lax.broadcasted_iota(jnp.int32, (rows, width), 0) + (core * ROWS + first)
        return ids.astype(F32)

    state = {}

    def near_1(key, axis, half):
        me, first, rest = here[axis], [group(), group()], group()
        remote(half(me, 0), half(me, 0), axis, 1, first[0])
        remote(half(me, 1), half(me, 1), axis, 3, first[1])
        remote(half(me, 1), half(me, 1), axis, 1, rest)
        remote(half(me, 0), half(me, 0), axis, 3, rest)
        state[key] = first, rest

    def near_2(key, n, axis, half):
        first, rest = state[key]
        owner = step(axis, (3, 1)[n])
        arrive(first[n])
        remote(half(owner, n), half(owner, n), axis, (1, 3)[n], rest)

    def sums_1(key, axis, half, far, landing):
        opposite, left, right = step(axis, 2), step(axis, 3), step(axis, 1)
        first, rest = [group(), group()], group()
        remote(half(opposite, 0), far.at[0], axis, 1, first[0])
        remote(half(opposite, 1), far.at[1], axis, 3, first[1])
        remote(half(right, 1), landing(0, 1), axis, 1, rest)
        remote(half(left, 0), landing(1, 0), axis, 3, rest)
        state[key] = first, rest

    def sums_2(key, n, axis, half, far, landing):
        first, rest = state[key]
        arrive(first[n])
        ref = half(step(axis, (1, 3)[n]), n)
        ref[...] = added(ref[...], [far[n]])
        remote(ref, landing(n, n), axis, (1, 3)[n], rest)

    def added(own, others):
        total = own.astype(F32)
        for other in others:
            total += other.astype(F32)
        return total.astype(BF16)

    def a_rows(k):
        return pl.ds(k * CH, AROWS[k])

    def b_rows(k):
        return pl.ds(k * CH + AROWS[k], AROWS[k])

    def c_rows(k, i):
        q = CROWS[k] // RING
        return pl.ds(pl.multiple_of(k * CH + 2 * AROWS[k] + i * q, 16), q)

    def a_half(ref, k):
        return lambda i, h: ref.at[2 * h:2 * h + 2, a_rows(k), cols(i)]

    def b_half(ref, k):
        a = AROWS[k]
        return lambda i, h: ref.at[i, pl.ds(k * CH + a + h * (a // 2), a // 2), :]

    def c_half(ref, k):
        return lambda i, h: ref.at[2 * h:2 * h + 2, c_rows(k, i), :]

    def a_land(k):
        return lambda n, h: m["a_in", k].at[n, 2 * h:2 * h + 2]

    def b_land(k):
        a = AROWS[k]
        return lambda n, h: m["b_in", k].at[n, h * (a // 2):(h + 1) * (a // 2), :]

    def c_land(k):
        return lambda n, h: m["c_in", k].at[n, 2 * h:2 * h + 2]

    def compact_rows(first, rows):
        total = jnp.zeros((rows, DS), F32)
        ids = row_ids(first, rows, L)
        for b in range(8):
            match = ids == (starts[b] + meta[b, 0:1, 0:L])
            total += jnp.dot(match.astype(F32).astype(BF16), raw[b], preferred_element_type=F32)
        return total.astype(BF16)

    def c_gather_1(k):
        q = CROWS[k] // RING
        x_buf[x, c_rows(k, z), cols(y)] = compact_rows(k * CH + 2 * AROWS[k] + z * q, q)
        if Y_FIRST[k]:
            state["c", k] = gather("y", lambda i: x_buf.at[x, c_rows(k, z), cols(i)])
        else:
            state["c", k] = gather("x", lambda i: x_buf.at[i, c_rows(k, z), cols(y)])

    def c_gather_2(k):
        arrive(state["c", k])
        if Y_FIRST[k]:
            state["c", k] = gather("x", lambda i: x_buf.at[i, c_rows(k, z), :])
        else:
            state["c", k] = gather("y", lambda i: x_buf.at[:, c_rows(k, z), cols(i)])

    def c_gather_3(k):
        arrive(state["c", k])
        near_1(("c", k), "z", c_half(x_buf, k))

    def c_gather_4(k, n):
        near_2(("c", k), n, "z", c_half(x_buf, k))

    def ab_gather_1(k):
        a = AROWS[k]
        x_buf[x, k * CH:k * CH + 2 * a, cols(y)] = compact_rows(k * CH, 2 * a)
        state["a", k] = gather("x", lambda i: x_buf.at[i, a_rows(k), cols(y)])
        state["b", k] = gather("y", lambda i: x_buf.at[x, b_rows(k), cols(i)])

    def a_gather_2(k):
        arrive(state["a", k])
        near_1(("a", k), "y", a_half(x_buf, k))

    def b_gather_2(k):
        arrive(state["b", k])
        near_1(("b", k), "x", b_half(x_buf, k))

    def a_gather_3(k, n):
        near_2(("a", k), n, "y", a_half(x_buf, k))

    def b_gather_3(k, n):
        near_2(("b", k), n, "x", b_half(x_buf, k))

    def gathered(k):
        for route in ("a", "b", "c"):
            arrive(state[route, k][1])

    def weights(k):
        own_copy.wait()
        w_copy.wait()

    def tables(k):
        for first in range(k * CH, k * CH + CH, 128):
            ids = row_ids(first, 128, L)
            target = jnp.zeros((128, L), F32)
            for b in range(8):
                match = ids == (starts[b] + meta[b, 0:1, 0:L])
                target += jnp.where(match, meta[b, 1:2, 0:L], 0.0)
            m["target"][first:first + 128, :] = jnp.broadcast_to(jnp.sum(target, axis=1, keepdims=True), (128, 128))
            ids = row_ids(first, 128, 128)
            weight = jnp.zeros((128, 128), F32)
            for b in range(8):
                low, size = starts[b][:, :128], counts[b][:, :128]
                weight += jnp.where((ids >= low) & (ids < low + size), jnp.float32(L) / size, 0.0)
            m["weight"][first:first + 128, :] = weight

    lane = lax.broadcasted_iota(jnp.int32, (CH, 128), 1)

    def scores(k, part):
        r = k * CH
        for n in range(part * WP // 2, (part + 1) * WP // 2, 256):
            total = jnp.zeros((CH, 256), F32)
            for i in range(RING):
                total += lax.dot_general(
                    x_buf[i, r:r + CH, :], w_buf[n:n + 256, i * DX:(i + 1) * DX], (((1,), (1,)), ((), ())),
                    preferred_element_type=F32,
                )
            s_buf[k, :, n:n + 256] = total

    def stats(k):
        tail = jnp.where(lane < WC - 7 * 128, s_buf[k, :, 7 * 128:8 * 128], -jnp.inf)
        s_buf[k, :, 7 * 128:8 * 128] = tail
        top = tail
        for t in range(7):
            top = jnp.maximum(top, s_buf[k, :, t * 128:(t + 1) * 128])
        top = jnp.max(top, axis=1, keepdims=True)
        total = jnp.zeros((CH, 128), F32)
        for t in range(8):
            e = jnp.exp(s_buf[k, :, t * 128:(t + 1) * 128] - top)
            s_buf[k, :, t * 128:(t + 1) * 128] = e
            total += e
        total = jnp.sum(total, axis=1, keepdims=True)
        both = jnp.where(lane == 0, top, total)
        st_buf[k, 0] = both.T[0:8]
        send_stats(k, 0)

    axes = ("x", "y", "z")

    def send_stats(k, n):
        to = group()
        for d in (1, 3, 2):
            remote(st_buf.at[k, n], st_in.at[k, n, d - 1], axes[n], d, to)
        state["stats", k] = to

    def merge_stats(k, n):
        arrive(state["stats", k])
        parts = [st_buf[k, n]] + [st_in[k, n, d] for d in range(3)]
        top = parts[0][0:1]
        for part in parts[1:]:
            top = jnp.maximum(top, part[0:1])
        total = jnp.zeros((1, CH), F32)
        for part in parts:
            total += part[1:2] * jnp.exp(part[0:1] - top)
        rows = lax.broadcasted_iota(jnp.int32, (8, CH), 0)
        st_buf[k, n + 1] = jnp.where(rows == 0, top, total)
        if n < 2:
            send_stats(k, n + 1)

    def gradients(k):
        r = k * CH
        own, whole = st_buf[k, 0], st_buf[k, 3]
        scale = jnp.exp(own[0:1] - whole[0:1]) / whole[1:2]
        scale = jnp.broadcast_to(scale, (128, CH)).T
        weight = m["weight"][r:r + CH, :]
        target = m["target"][r:r + CH, :]
        first = (vocab * 8 + z * 2) * WR
        for t in range(8):
            ids = (lane + (first + t * 128)).astype(F32)
            onehot = jnp.where(ids == target, 1.0 - smoothing, 0.0)
            probs = s_buf[k, :, t * 128:(t + 1) * 128] * scale
            d_buf[:, t * 128:(t + 1) * 128] = (weight * (probs - onehot - smoothing / VOCAB)).astype(BF16)

    def products(k, part):
        r = k * CH

        def body(i, carry):
            for j in range(RING):
                p_buf[i, r:r + CH, j * DS:(j + 1) * DS] = jnp.dot(
                    d_buf[...], w_buf[:, cols(i * RING + j)], preferred_element_type=F32
                ).astype(BF16)
            return carry

        lax.fori_loop(2 * part, 2 * part + 2, body, 0)

    def c_scatter_1(k):
        sums_1(("c", k), "z", c_half(p_buf, k), m["c_far", k], c_land(k))

    def a_scatter_1(k):
        sums_1(("a", k), "y", a_half(p_buf, k), m["a_far", k], a_land(k))

    def b_scatter_1(k):
        sums_1(("b", k), "x", b_half(p_buf, k), m["b_far", k], b_land(k))

    def c_scatter_2(k, n):
        sums_2(("c", k), n, "z", c_half(p_buf, k), m["c_far", k], c_land(k))

    def a_scatter_2(k, n):
        sums_2(("a", k), n, "y", a_half(p_buf, k), m["a_far", k], a_land(k))

    def b_scatter_2(k, n):
        sums_2(("b", k), n, "x", b_half(p_buf, k), m["b_far", k], b_land(k))

    def c_scatter_3(k):
        arrive(state["c", k][1])
        c_sum, c_in = m["c_sum", k], m["c_in", k]
        for i in range(RING):
            c_sum[i] = added(p_buf[i, c_rows(k, z), :], [c_in[0, i], c_in[1, i]])
        if Y_FIRST[k]:
            state["c", k] = scatter("x", lambda i: c_sum.at[i], m["c_in2", k])
        else:
            state["c", k] = scatter("y", lambda i: c_sum.at[:, :, cols(i)], m["c_in2", k])

    def a_scatter_3(k):
        arrive(state["a", k][1])
        a_sum, a_in = m["a_sum", k], m["a_in", k]
        for i in range(RING):
            a_sum[i] = added(p_buf[i, a_rows(k), cols(y)], [a_in[0, i], a_in[1, i]])
        state["a", k] = scatter("x", lambda i: a_sum.at[i], m["a_in2", k])

    def b_scatter_3(k):
        arrive(state["b", k][1])
        b_sum, b_in = m["b_sum", k], m["b_in", k]
        for h in range(0, AROWS[k], 32):
            own = p_buf[x, k * CH + AROWS[k] + h:k * CH + AROWS[k] + h + 32, :]
            b_sum[h:h + 32, :] = added(own, [b_in[0, h:h + 32, :], b_in[1, h:h + 32, :]])
        state["b", k] = scatter("y", lambda i: b_sum.at[:, cols(i)], m["b_in2", k])

    def c_scatter_4(k):
        arrive(state["c", k])
        c_sum, c_in2, c_sum2 = m["c_sum", k], m["c_in2", k], m["c_sum2", k]
        if Y_FIRST[k]:
            c_sum2[...] = added(c_sum[x], [c_in2[d] for d in range(3)])
            state["c", k] = scatter("y", lambda i: c_sum2.at[:, cols(i)], m["c_in3", k])
        else:
            for i in range(RING):
                c_sum2[i] = added(c_sum[i, :, cols(y)], [c_in2[d, i] for d in range(3)])
            state["c", k] = scatter("x", lambda i: c_sum2.at[i], m["c_in3", k])

    def ab_scatter_4(k):
        n, ab = AROWS[k], m["ab", k]
        arrive(state["a", k])
        ab[0:n, :] = added(m["a_sum", k][x], [m["a_in2", k][d] for d in range(3)])
        arrive(state["b", k])
        ab[n:2 * n, :] = added(m["b_sum", k][:, cols(y)], [m["b_in2", k][d] for d in range(3)])
        state["ab", k] = scatter(
            "z", lambda i: ab.at[pl.ds(pl.multiple_of(i * (n // 2), 16), n // 2), :], m["ab_in", k])

    def spread(k):
        n = AROWS[k] // 2
        g, c_sum2 = m["g", k], m["c_sum2", k]
        arrive(state["c", k])
        own = c_sum2[:, cols(y)] if Y_FIRST[k] else c_sum2[x]
        g[core, z, n:PART, :] = added(own, [m["c_in3", k][d] for d in range(3)])
        arrive(state["ab", k])
        own = m["ab", k][pl.ds(pl.multiple_of(z * n, 16), n), :]
        g[core, z, 0:n, :] = added(own, [m["ab_in", k][d] for d in range(3)])
        near, other = [group() for _ in range(3)], group()
        block = g.at[core, z]
        for i, d in enumerate((1, 3, 2)):
            remote(block, block, "z", d, near[i])
        remote(block, block, "core", 0, other)
        state["g", k] = near, other

    def spread_over(k):
        near, other = state["g", k]
        for i, d in enumerate((1, 3, 2)):
            arrive(near[i])
            block = m["g", k].at[core, step("z", 4 - d)]
            remote(block, block, "core", 0, other)

    def selection(k):
        start = jnp.zeros((1, L), F32)
        for b in range(8):
            start += jnp.where(dp == b, starts[b], 0.0)
        where = start + rank
        where = jnp.broadcast_to(where, (128, L)).T
        ids = lax.broadcasted_iota(jnp.int32, (L, 128), 1)
        for side in range(2):
            for k in range(CHUNKS):
                n, q = AROWS[k] // 2, CROWS[k] // RING
                for t in range(2):
                    i = ids & (PART - 1)
                    zi = (ids >> 6) + 2 * t
                    rows = jnp.where(i < n, zi * n + i, 4 * n + zi * q + i - n) + (side * ROWS + k * CH)
                    first = side * ROWS + k * CH + t * 128
                    sel[:, first:first + 128] = (where == rows.astype(F32)).astype(F32).astype(BF16)

    def place_rows(k):
        arrive(state["g", k][1])
        total = state.get("total", 0.0)
        for side in range(2):
            first = side * ROWS + k * CH
            total += jnp.dot(
                sel[:, first:first + CH], m["g", k][side].reshape(CH, DS), preferred_element_type=F32
            )
        state["total"] = total

    for run, *at in (
    (c_gather_1, 0), (c_gather_1, 1), (ab_gather_1, 0), (c_gather_1, 2), (tables, 2), (c_gather_2, 0),
        (c_gather_2, 1), (ab_gather_1, 2), (tables, 0), (c_gather_2, 2), (selection, 0), (ab_gather_1, 1),
        (c_gather_3, 0), (b_gather_2, 0), (a_gather_2, 0), (c_gather_3, 1), (b_gather_2, 1),
        (b_gather_3, 0, 1), (a_gather_3, 0, 0), (a_gather_3, 0, 1), (c_gather_4, 0, 1), (c_gather_4, 0, 0),
        (a_gather_2, 1), (b_gather_3, 0, 0), (b_gather_3, 1, 0), (c_gather_4, 1, 0), (c_gather_4, 1, 1),
        (tables, 1), (weights, 0), (b_gather_3, 1, 1), (b_gather_2, 2), (c_gather_3, 2), (a_gather_3, 1, 0),
        (a_gather_3, 1, 1), (a_gather_2, 2), (gathered, 0), (scores, 0, 1), (scores, 0, 0), (stats, 0),
        (b_gather_3, 2, 0), (b_gather_3, 2, 1), (c_gather_4, 2, 1), (gathered, 1), (c_gather_4, 2, 0),
        (a_gather_3, 2, 0), (a_gather_3, 2, 1), (scores, 1, 0), (scores, 1, 1), (merge_stats, 0, 0),
        (gathered, 2), (stats, 1), (scores, 2, 1), (merge_stats, 0, 1), (scores, 2, 0), (stats, 2),
        (merge_stats, 1, 0), (merge_stats, 0, 2), (gradients, 0), (products, 0, 0), (merge_stats, 2, 0),
        (merge_stats, 1, 1), (products, 0, 1), (c_scatter_1, 0), (a_scatter_1, 0), (b_scatter_1, 0),
        (merge_stats, 2, 1), (merge_stats, 1, 2), (gradients, 1), (products, 1, 1), (products, 1, 0),
        (a_scatter_2, 0, 1), (b_scatter_2, 0, 1), (a_scatter_1, 1), (c_scatter_1, 1), (merge_stats, 2, 2),
        (b_scatter_2, 0, 0), (a_scatter_2, 0, 0), (b_scatter_1, 1), (gradients, 2), (products, 2, 0),
        (products, 2, 1), (a_scatter_1, 2), (b_scatter_1, 2), (a_scatter_2, 1, 0), (b_scatter_2, 1, 0),
        (c_scatter_1, 2), (c_scatter_2, 1, 1), (a_scatter_2, 1, 1), (c_scatter_2, 1, 0), (b_scatter_3, 0),
        (b_scatter_2, 1, 1), (c_scatter_2, 0, 0), (a_scatter_3, 0), (b_scatter_2, 2, 0), (a_scatter_2, 2, 0),
        (a_scatter_2, 2, 1), (c_scatter_2, 0, 1), (b_scatter_2, 2, 1), (c_scatter_2, 2, 0), (c_scatter_3, 1),
        (c_scatter_3, 0), (c_scatter_2, 2, 1), (a_scatter_3, 1), (ab_scatter_4, 0), (a_scatter_3, 2),
        (b_scatter_3, 1), (b_scatter_3, 2), (c_scatter_3, 2), (c_scatter_4, 1), (c_scatter_4, 0),
        (ab_scatter_4, 1), (ab_scatter_4, 2), (c_scatter_4, 2), (spread, 0), (spread, 1), (spread, 2),
        (spread_over, 0), (spread_over, 1), (spread_over, 2), (place_rows, 1), (place_rows, 0),
        (place_rows, 2),
    ):
        run(*at)
    out[...] = state["total"].astype(BF16)
    for i, units in sends:
        settle(send_sem.at[i], units)


def local(hidden, positions, targets, counts, out_weight):
    vmem = pl.BlockSpec(memory_space=pltpu.VMEM)
    return pl.pallas_call(
        kernel,
        out_shape=jax.ShapeDtypeStruct((L, DS), BF16),
        in_specs=[vmem, vmem, vmem, pl.BlockSpec(memory_space=pltpu.SMEM), pl.BlockSpec(memory_space=pl.ANY)],
        out_specs=vmem,
        scratch_shapes=[
            *(pltpu.VMEM(shape, dtype) for shape, dtype in scratch().values()),
            pltpu.SemaphoreType.DMA((3,)),
            pltpu.SemaphoreType.DMA((SENDS,)),
            pltpu.SemaphoreType.DMA((ARRIVALS,)),
        ],
        compiler_params=pltpu.CompilerParams(collective_id=0, has_side_effects=True, vmem_limit_bytes=56 << 20),
        cost_estimate=pl.CostEstimate(flops=4 * ROWS * WC * D, bytes_accessed=2 * WR * D, transcendentals=ROWS * WC),
        name="masked_row_gradient",
    )(hidden[0], positions, targets, counts, out_weight)[None]


def solution(mesh):
    return jax.shard_map(
        local,
        mesh=mesh,
        in_specs=(
            P("dp", None, "vocab"),
            P("dp", None),
            P("dp", None),
            P("dp"),
            P(("vocab", "dp"), None),
        ),
        out_specs=P("dp", None, "vocab"),
        check_vma=False,
    )
```

time: 124 us -> 105 us (0.85)
  Pallas kernels: 122 us -> 103 us
    pallas_call x1, Pallas kernels: 122 us -> 103 us  [local(): pl.pallas_call(kernel, out_shape=jax.ShapeDtypeStruct((L, DS), BF16), in_...]
where the time goes in v3:
time: 105 us
  Pallas kernels  103 us (98%)
  local copies, waits for them, and re-layouts  1.62 us (2%)
    pallas_call x1, Pallas kernels, local(): pl.pallas_call(kernel, out_shape=jax.ShapeDtypeStruct((L, DS), BF16), in_...  103 us

profile of v3, /device:TPU:1, one launch (start us, length us, event | category | flops | bytes accessed | tf_op | source)
XLA Modules:
  0.0 105.2 jit_solution(10804612964598599958)
XLA Ops:
  0.7 102.9 %masked_row_gradient.1 = bf16[384,256]{1,0:T(8,128)(2,1)} custom-call(bf16[384,256]{1,0:T(8,128)(2,1)} %bitcast.3, s32[1,384]{1,0:T(1,128)} %pos.1, s32[1,384]{1,0:T(1,128)} %tgt.1, s32[1]{0:T(128)S(6)} %copy.7.cnt, bf16[496,4096]{1,0:T(8,128)(2,1)} %w_in.1), custom_call_target="tpu_custom_call" | custom-call | flops 12482248704 | bytes 4063232 | tf_op jit(solution)/shard_map/masked_row_gradient/pallas_call | solution.py:565
  103.6 1.6 %copy.8 = bf16[1,384,256]{2,1,0:T(8,128)(2,1)} copy(bf16[1,384,256]{2,1,0:T(8,128)(2,1)} %bitcast.2) | data formatting | bytes 393216

commit v4 on v3

--- a/solution.py
+++ b/solution.py
@@ -26,10 +26,10 @@
 Y_FIRST = (True, False, True)
 PART = CH // RING
 DEAD = 1.0e6
-ARRIVALS = 128
-SENDS = 32
-UNIT = 16 * DS * 2
-UNITS = 128
+ARRIVALS = 108
+SENDS = 15
+UNIT = 4096
+UNITS = 256
 
 
 def scratch():
@@ -39,9 +39,10 @@
         "w": ((WP, D), BF16),
         "s": ((CHUNKS, CH, WP), F32),
         "d": ((CH, WP), BF16),
-        "raw": ((8, L, DS), BF16),
-        "unit": ((UNITS, 16, DS), BF16),
-        "meta": ((8, 8, 512), F32),
+        "raw": ((2, RING, L, DS), BF16),
+        "unit": ((UNITS, 8, 128), F32),
+        "codes": ((2, RING, 8, 128), jnp.int32),
+        "meta": ((8, 8, L), F32),
         "target": ((ROWS, 128), F32),
         "weight": ((ROWS, 128), F32),
         "sel": ((L, 2 * ROWS), BF16),
@@ -76,7 +77,7 @@
     m = dict(zip(scratch(), refs))
     w_sem, send_sem, recv_sem = refs[len(m):]
     x_buf, p_buf, w_buf, s_buf, d_buf = m["x"], m["p"], m["w"], m["s"], m["d"]
-    raw, meta, sel, st_buf, st_in = m["raw"], m["meta"], m["sel"], m["st"], m["st_in"]
+    codes, raw, meta, sel, st_buf, st_in = m["codes"], m["raw"], m["meta"], m["sel"], m["st"], m["st_in"]
     dp, vocab = lax.axis_index("dp"), lax.axis_index("vocab")
     z, core = lax.div(dp, 2), lax.rem(dp, 2)
     x, y = lax.div(vocab, RING), lax.rem(vocab, RING)
@@ -148,10 +149,8 @@
     pl.semaphore_signal(barrier, inc=1, device_id=device("core", 0), device_id_type=MESH)
 
     own_rows = pl.ds(pl.multiple_of(core * WR, 16), WR)
-    own_copy = pltpu.make_async_copy(w_in, w_buf.at[own_rows], w_sem.at[0])
-    own_copy.start()
-
-    raw[dp] = hid[...]
+    raw_copy = pltpu.make_async_copy(hid, raw.at[core, z], w_sem.at[3])
+    raw_copy.start()
     count = jnp.full((1, L), cnt[0], jnp.int32).astype(F32)
     place = lax.broadcasted_iota(jnp.int32, (L, L), 0) == pos[...]
     entry = lax.broadcasted_iota(jnp.int32, (8, L), 1)
@@ -159,27 +158,44 @@
     digits = jnp.where(half == 0, lax.div(entry, 128), lax.rem(entry, 128)).astype(F32).astype(BF16)
     found = lax.dot_general(digits, place.astype(F32).astype(BF16), (((1,), (1,)), ((), ())), preferred_element_type=F32)
     rank = found[0:1] * 128.0 + found[1:2]
-    rank = jnp.where(rank < count, rank, DEAD)
-    meta[dp] = jnp.zeros((8, 512), F32)
-    meta[dp, 0:1, 0:L] = rank
-    meta[dp, 1:2, 0:L] = tgt[...].astype(F32)
-    meta[dp, 2:3, 0:L] = count
+    code = tgt[...] * 1024 + jnp.where(rank < count, rank, 1023.0).astype(jnp.int32)
+    for n in range(3):
+        codes[core, z, n:n + 1, :] = code[:, n * 128:(n + 1) * 128]
     w_buf[WC:WP, :] = jnp.zeros((WP - WC, D), BF16)
 
     pl.semaphore_wait(barrier, 10)
 
-    near = [group() for _ in range(3)]
+    def raw_half(i, h):
+        return raw.at[core, i, :, h * 128:(h + 1) * 128]
+
+    def over(block):
+        remote(block, block, "core", 0, other)
+
+    def below(i):
+        return codes.at[core, i]
+
+    raw_copy.wait()
     other = group()
-    for n, d in enumerate((1, 3, 2)):
-        remote(raw.at[dp], raw.at[dp], "z", d, near[n])
-        remote(meta.at[dp], meta.at[dp], "z", d, near[n])
-    remote(raw.at[dp], raw.at[dp], "core", 0, other)
-    remote(meta.at[dp], meta.at[dp], "core", 0, other)
-    for n, d in enumerate((1, 3, 2)):
-        source = step("z", 4 - d) * 2 + core
-        arrive(near[n])
-        remote(raw.at[source], raw.at[source], "core", 0, other)
-        remote(meta.at[source], meta.at[source], "core", 0, other)
+    near_codes = gather("z", below)
+    first, second, far = [group(), group()], group(), group()
+    for h, d, to in ((0, 1, first[0]), (1, 3, first[1]), (1, 1, second), (0, 3, second)):
+        remote(raw_half(z, h), raw_half(z, h), "z", d, to)
+    over(raw.at[core, z])
+    own_copy = pltpu.make_async_copy(w_in, w_buf.at[own_rows], w_sem.at[0])
+    own_copy.start()
+
+    arrive(near_codes)
+    over(codes.at[core])
+    left, right, opposite = step("z", 3), step("z", 1), step("z", 2)
+    for owner, h, d in ((left, 0, 1), (right, 1, 3)):
+        arrive(first[h])
+        remote(raw_half(owner, h), raw_half(owner, h), "z", d, far)
+        over(raw_half(owner, h))
+    arrive(second)
+    over(raw_half(left, 1))
+    over(raw_half(right, 0))
+    arrive(far)
+    over(raw.at[core, opposite])
     w_copy = pltpu.make_async_remote_copy(
         src_ref=w_in, dst_ref=w_buf.at[own_rows], send_sem=w_sem.at[1], recv_sem=w_sem.at[2],
         device_id=device("core", 0), device_id_type=MESH,
@@ -187,10 +203,17 @@
     w_copy.start()
     arrive(other)
 
-    counts = [meta[b, 2:3, 0:L] for b in range(8)]
-    starts = [jnp.zeros((1, L), F32)]
-    for b in range(7):
-        starts.append(starts[-1] + counts[b])
+    start = jnp.zeros((1, 1), F32)
+    for b in range(8):
+        code = jnp.concatenate([codes[b % 2, b // 2, n:n + 1, :] for n in range(3)], axis=1)
+        rank = code & 1023
+        live = rank < 1023
+        size = jnp.sum(live.astype(F32), axis=1, keepdims=True)
+        meta[b, 0:1, :] = jnp.where(live, start + rank.astype(F32), DEAD)
+        meta[b, 1:2, :] = (code >> 10).astype(F32)
+        meta[b, 2:3, :] = jnp.broadcast_to(size, (1, L))
+        meta[b, 3:4, :] = jnp.broadcast_to(start, (1, L))
+        start += size
 
     def row_ids(first, rows, width):
         ids = lax.broadcasted_iota(jnp.int32, (rows, width), 0) + (core * ROWS + first)
@@ -268,8 +291,8 @@
         total = jnp.zeros((rows, DS), F32)
         ids = row_ids(first, rows, L)
         for b in range(8):
-            match = ids == (starts[b] + meta[b, 0:1, 0:L])
-            total += jnp.dot(match.astype(F32).astype(BF16), raw[b], preferred_element_type=F32)
+            match = ids == meta[b, 0:1, :]
+            total += jnp.dot(match.astype(F32).astype(BF16), raw[b % 2, b // 2], preferred_element_type=F32)
         return total.astype(BF16)
 
     def c_gather_1(k):
@@ -327,13 +350,13 @@
             ids = row_ids(first, 128, L)
             target = jnp.zeros((128, L), F32)
             for b in range(8):
-                match = ids == (starts[b] + meta[b, 0:1, 0:L])
-                target += jnp.where(match, meta[b, 1:2, 0:L], 0.0)
+                match = ids == meta[b, 0:1, :]
+                target += jnp.where(match, meta[b, 1:2, :], 0.0)
             m["target"][first:first + 128, :] = jnp.broadcast_to(jnp.sum(target, axis=1, keepdims=True), (128, 128))
             ids = row_ids(first, 128, 128)
             weight = jnp.zeros((128, 128), F32)
             for b in range(8):
-                low, size = starts[b][:, :128], counts[b][:, :128]
+                low, size = meta[b, 3:4, 0:128], meta[b, 2:3, 0:128]
                 weight += jnp.where((ids >= low) & (ids < low + size), jnp.float32(L) / size, 0.0)
             m["weight"][first:first + 128, :] = weight
 
@@ -502,10 +525,7 @@
             remote(block, block, "core", 0, other)
 
     def selection(k):
-        start = jnp.zeros((1, L), F32)
-        for b in range(8):
-            start += jnp.where(dp == b, starts[b], 0.0)
-        where = start + rank
+        where = meta[dp, 0:1, :]
         where = jnp.broadcast_to(where, (128, L)).T
         ids = lax.broadcasted_iota(jnp.int32, (L, 128), 1)
         for side in range(2):
@@ -529,30 +549,29 @@
         state["total"] = total
 
     for run, *at in (
-    (c_gather_1, 0), (c_gather_1, 1), (ab_gather_1, 0), (c_gather_1, 2), (tables, 2), (c_gather_2, 0),
-        (c_gather_2, 1), (ab_gather_1, 2), (tables, 0), (c_gather_2, 2), (selection, 0), (ab_gather_1, 1),
-        (c_gather_3, 0), (b_gather_2, 0), (a_gather_2, 0), (c_gather_3, 1), (b_gather_2, 1),
-        (b_gather_3, 0, 1), (a_gather_3, 0, 0), (a_gather_3, 0, 1), (c_gather_4, 0, 1), (c_gather_4, 0, 0),
-        (a_gather_2, 1), (b_gather_3, 0, 0), (b_gather_3, 1, 0), (c_gather_4, 1, 0), (c_gather_4, 1, 1),
-        (tables, 1), (weights, 0), (b_gather_3, 1, 1), (b_gather_2, 2), (c_gather_3, 2), (a_gather_3, 1, 0),
-        (a_gather_3, 1, 1), (a_gather_2, 2), (gathered, 0), (scores, 0, 1), (scores, 0, 0), (stats, 0),
-        (b_gather_3, 2, 0), (b_gather_3, 2, 1), (c_gather_4, 2, 1), (gathered, 1), (c_gather_4, 2, 0),
-        (a_gather_3, 2, 0), (a_gather_3, 2, 1), (scores, 1, 0), (scores, 1, 1), (merge_stats, 0, 0),
-        (gathered, 2), (stats, 1), (scores, 2, 1), (merge_stats, 0, 1), (scores, 2, 0), (stats, 2),
-        (merge_stats, 1, 0), (merge_stats, 0, 2), (gradients, 0), (products, 0, 0), (merge_stats, 2, 0),
-        (merge_stats, 1, 1), (products, 0, 1), (c_scatter_1, 0), (a_scatter_1, 0), (b_scatter_1, 0),
-        (merge_stats, 2, 1), (merge_stats, 1, 2), (gradients, 1), (products, 1, 1), (products, 1, 0),
-        (a_scatter_2, 0, 1), (b_scatter_2, 0, 1), (a_scatter_1, 1), (c_scatter_1, 1), (merge_stats, 2, 2),
-        (b_scatter_2, 0, 0), (a_scatter_2, 0, 0), (b_scatter_1, 1), (gradients, 2), (products, 2, 0),
-        (products, 2, 1), (a_scatter_1, 2), (b_scatter_1, 2), (a_scatter_2, 1, 0), (b_scatter_2, 1, 0),
-        (c_scatter_1, 2), (c_scatter_2, 1, 1), (a_scatter_2, 1, 1), (c_scatter_2, 1, 0), (b_scatter_3, 0),
-        (b_scatter_2, 1, 1), (c_scatter_2, 0, 0), (a_scatter_3, 0), (b_scatter_2, 2, 0), (a_scatter_2, 2, 0),
-        (a_scatter_2, 2, 1), (c_scatter_2, 0, 1), (b_scatter_2, 2, 1), (c_scatter_2, 2, 0), (c_scatter_3, 1),
-        (c_scatter_3, 0), (c_scatter_2, 2, 1), (a_scatter_3, 1), (ab_scatter_4, 0), (a_scatter_3, 2),
-        (b_scatter_3, 1), (b_scatter_3, 2), (c_scatter_3, 2), (c_scatter_4, 1), (c_scatter_4, 0),
-        (ab_scatter_4, 1), (ab_scatter_4, 2), (c_scatter_4, 2), (spread, 0), (spread, 1), (spread, 2),
-        (spread_over, 0), (spread_over, 1), (spread_over, 2), (place_rows, 1), (place_rows, 0),
-        (place_rows, 2),
+        (c_gather_1, 1), (c_gather_1, 0), (ab_gather_1, 0), (c_gather_1, 2), (c_gather_2, 0), (c_gather_2, 1),
+        (ab_gather_1, 1), (b_gather_2, 0), (a_gather_2, 0), (c_gather_3, 0), (c_gather_2, 2), (ab_gather_1, 2),
+        (c_gather_3, 1), (weights, 0), (b_gather_3, 0, 1), (c_gather_4, 0, 1), (b_gather_3, 0, 0), (tables, 2),
+        (a_gather_3, 0, 1), (a_gather_3, 0, 0), (b_gather_2, 1), (a_gather_2, 1), (c_gather_4, 0, 0),
+        (c_gather_4, 1, 1), (tables, 0), (tables, 1), (c_gather_4, 1, 0), (c_gather_3, 2), (b_gather_3, 1, 0),
+        (b_gather_3, 1, 1), (gathered, 0), (a_gather_3, 1, 0), (a_gather_3, 1, 1), (a_gather_2, 2),
+        (b_gather_2, 2), (scores, 0, 1), (scores, 0, 0), (c_gather_4, 2, 0), (stats, 0), (c_gather_4, 2, 1),
+        (gathered, 1), (b_gather_3, 2, 1), (b_gather_3, 2, 0), (a_gather_3, 2, 0), (a_gather_3, 2, 1),
+        (scores, 1, 0), (scores, 1, 1), (merge_stats, 0, 0), (stats, 1), (gathered, 2), (scores, 2, 0),
+        (merge_stats, 0, 1), (scores, 2, 1), (merge_stats, 1, 0), (stats, 2), (merge_stats, 0, 2),
+        (gradients, 0), (products, 0, 0), (merge_stats, 1, 1), (products, 0, 1), (b_scatter_1, 0),
+        (merge_stats, 2, 0), (a_scatter_1, 0), (c_scatter_1, 0), (merge_stats, 1, 2), (gradients, 1),
+        (products, 1, 1), (merge_stats, 2, 1), (b_scatter_2, 0, 0), (b_scatter_2, 0, 1), (a_scatter_2, 0, 0),
+        (a_scatter_2, 0, 1), (products, 1, 0), (b_scatter_1, 1), (merge_stats, 2, 2), (a_scatter_1, 1),
+        (gradients, 2), (c_scatter_1, 1), (products, 2, 1), (b_scatter_3, 0), (a_scatter_3, 0),
+        (products, 2, 0), (a_scatter_1, 2), (b_scatter_1, 2), (a_scatter_2, 1, 0), (c_scatter_2, 0, 0),
+        (c_scatter_2, 1, 1), (b_scatter_2, 1, 1), (b_scatter_2, 1, 0), (c_scatter_2, 1, 0), (a_scatter_2, 1, 1),
+        (selection, 0), (a_scatter_2, 2, 1), (c_scatter_2, 0, 1), (b_scatter_2, 2, 1), (c_scatter_1, 2),
+        (a_scatter_2, 2, 0), (b_scatter_2, 2, 0), (c_scatter_3, 1), (c_scatter_3, 0), (c_scatter_2, 2, 1),
+        (a_scatter_3, 1), (c_scatter_2, 2, 0), (b_scatter_3, 1), (a_scatter_3, 2), (ab_scatter_4, 0),
+        (b_scatter_3, 2), (c_scatter_3, 2), (c_scatter_4, 0), (c_scatter_4, 1), (ab_scatter_4, 1),
+        (ab_scatter_4, 2), (c_scatter_4, 2), (spread, 0), (spread, 1), (spread, 2), (spread_over, 0),
+        (spread_over, 1), (spread_over, 2), (place_rows, 0), (place_rows, 1), (place_rows, 2),
     ):
         run(*at)
     out[...] = state["total"].astype(BF16)
@@ -561,15 +580,15 @@
 
 
 def local(hidden, positions, targets, counts, out_weight):
-    vmem = pl.BlockSpec(memory_space=pltpu.VMEM)
+    vmem, far = pl.BlockSpec(memory_space=pltpu.VMEM), pl.BlockSpec(memory_space=pl.ANY)
     return pl.pallas_call(
         kernel,
         out_shape=jax.ShapeDtypeStruct((L, DS), BF16),
-        in_specs=[vmem, vmem, vmem, pl.BlockSpec(memory_space=pltpu.SMEM), pl.BlockSpec(memory_space=pl.ANY)],
+        in_specs=[far, vmem, vmem, pl.BlockSpec(memory_space=pltpu.SMEM), far],
         out_specs=vmem,
         scratch_shapes=[
             *(pltpu.VMEM(shape, dtype) for shape, dtype in scratch().values()),
-            pltpu.SemaphoreType.DMA((3,)),
+            pltpu.SemaphoreType.DMA((4,)),
             pltpu.SemaphoreType.DMA((SENDS,)),
             pltpu.SemaphoreType.DMA((ARRIVALS,)),
         ],

time: 105 us -> 103 us (0.981)
  Pallas kernels: 103 us -> 100 us
    pallas_call x1, Pallas kernels: 103 us -> 100 us  [local(): pl.pallas_call(kernel, out_shape=jax.ShapeDtypeStruct((L, DS), BF16), in_...]
where the time goes in v4:
time: 103 us; the launch traced here: 102 us
  Pallas kernels  100 us (97%)
  local copies, waits for them, and re-layouts  1.62 us (2%)
    pallas_call x1, Pallas kernels, local(): pl.pallas_call(kernel, out_shape=jax.ShapeDtypeStruct((L, DS), BF16), in_...  100 us

profile of v4, /device:TPU:1, one launch (start us, length us, event | category | flops | bytes accessed | tf_op | source)
XLA Modules:
  0.0 102.5 jit_solution(13618459967480585277)
XLA Ops:
  0.7 100.2 %masked_row_gradient.1 = bf16[384,256]{1,0:T(8,128)(2,1)} custom-call(bf16[384,256]{1,0:T(8,128)(2,1)} %bitcast.3, s32[1,384]{1,0:T(1,128)} %pos.1, s32[1,384]{1,0:T(1,128)} %tgt.1, s32[1]{0:T(128)S(6)} %copy.7.cnt, bf16[496,4096]{1,0:T(8,128)(2,1)} %w_in.1), custom_call_target="tpu_custom_call" | custom-call | flops 12482248704 | bytes 4063232 | tf_op jit(solution)/shard_map/masked_row_gradient/pallas_call | solution.py:584
  100.9 1.6 %copy.8 = bf16[1,384,256]{2,1,0:T(8,128)(2,1)} copy(bf16[1,384,256]{2,1,0:T(8,128)(2,1)} %bitcast.2) | data formatting | bytes 393216

commit v5 on v4

--- a/solution.py
+++ b/solution.py
@@ -24,9 +24,11 @@
 AROWS = (96, 64, 96)
 CROWS = (64, 128, 64)
 Y_FIRST = (True, False, True)
+NEAR_IN = (1, 2)
+NEAR_OUT = (0, 1)
 PART = CH // RING
 DEAD = 1.0e6
-ARRIVALS = 108
+ARRIVALS = 124
 SENDS = 15
 UNIT = 4096
 UNITS = 256
@@ -62,6 +64,8 @@
             ("b_sum", k): ((a, DX), BF16),
             ("c_sum", k): ((RING, q, DX), BF16),
             ("a_in2", k): ((3, a, DS), BF16),
+            ("a_far2", k): ((2, a // 2, DS), BF16),
+            ("b_far2", k): ((2, a // 2, DS), BF16),
             ("b_in2", k): ((3, a, DS), BF16),
             ("c_in2", k): ((3, q, DX) if Y_FIRST[k] else (3, RING, q, DS), BF16),
             ("c_sum2", k): ((q, DX) if Y_FIRST[k] else (RING, q, DS), BF16),
@@ -235,14 +239,14 @@
         arrive(first[n])
         remote(half(owner, n), half(owner, n), axis, (1, 3)[n], rest)
 
-    def sums_1(key, axis, half, far, landing):
+    def sums_1(key, parts, axis, half, far, landing):
         opposite, left, right = step(axis, 2), step(axis, 3), step(axis, 1)
-        first, rest = [group(), group()], group()
-        remote(half(opposite, 0), far.at[0], axis, 1, first[0])
-        remote(half(opposite, 1), far.at[1], axis, 3, first[1])
-        remote(half(right, 1), landing(0, 1), axis, 1, rest)
-        remote(half(left, 0), landing(1, 0), axis, 3, rest)
-        state[key] = first, rest
+        if key not in state:
+            state[key] = [group(), group()], group()
+        first, rest = state[key]
+        for n in parts:
+            remote(half(opposite, n), far.at[n], axis, (1, 3)[n], first[n])
+            remote(half((left, right)[n], n), landing(1 - n, n), axis, (3, 1)[n], rest)
 
     def sums_2(key, n, axis, half, far, landing):
         first, rest = state[key]
@@ -317,18 +321,36 @@
     def c_gather_4(k, n):
         near_2(("c", k), n, "z", c_half(x_buf, k))
 
+    def a_slice(k):
+        a = AROWS[k]
+        return lambda i, h: x_buf.at[i, pl.ds(k * CH + h * (a // 2), a // 2), cols(y)]
+
+    def b_slice(k):
+        a = AROWS[k]
+        return lambda i, h: x_buf.at[x, pl.ds(k * CH + a + h * (a // 2), a // 2), cols(i)]
+
     def ab_gather_1(k):
         a = AROWS[k]
         x_buf[x, k * CH:k * CH + 2 * a, cols(y)] = compact_rows(k * CH, 2 * a)
-        state["a", k] = gather("x", lambda i: x_buf.at[i, a_rows(k), cols(y)])
-        state["b", k] = gather("y", lambda i: x_buf.at[x, b_rows(k), cols(i)])
+        if k in NEAR_IN:
+            near_1(("a", k), "x", a_slice(k))
+            near_1(("b", k), "y", b_slice(k))
+        else:
+            state["a", k] = None, gather("x", lambda i: x_buf.at[i, a_rows(k), cols(y)])
+            state["b", k] = None, gather("y", lambda i: x_buf.at[x, b_rows(k), cols(i)])
+
+    def a_gather_1(k, n):
+        near_2(("a", k), n, "x", a_slice(k))
+
+    def b_gather_1(k, n):
+        near_2(("b", k), n, "y", b_slice(k))
 
     def a_gather_2(k):
-        arrive(state["a", k])
+        arrive(state["a", k][1])
         near_1(("a", k), "y", a_half(x_buf, k))
 
     def b_gather_2(k):
-        arrive(state["b", k])
+        arrive(state["b", k][1])
         near_1(("b", k), "x", b_half(x_buf, k))
 
     def a_gather_3(k, n):
@@ -438,26 +460,37 @@
 
         lax.fori_loop(2 * part, 2 * part + 2, body, 0)
 
-    def c_scatter_1(k):
-        sums_1(("c", k), "z", c_half(p_buf, k), m["c_far", k], c_land(k))
-
-    def a_scatter_1(k):
-        sums_1(("a", k), "y", a_half(p_buf, k), m["a_far", k], a_land(k))
+    def c_scatter_1(k, n):
+        sums_1(("c out", k), (n,), "z", c_half(p_buf, k), m["c_far", k], c_land(k))
+
+    def a_scatter_1(k, n):
+        sums_1(("a out", k), (n,), "y", a_half(p_buf, k), m["a_far", k], a_land(k))
 
     def b_scatter_1(k):
-        sums_1(("b", k), "x", b_half(p_buf, k), m["b_far", k], b_land(k))
+        sums_1(("b out", k), (0, 1), "x", b_half(p_buf, k), m["b_far", k], b_land(k))
 
     def c_scatter_2(k, n):
-        sums_2(("c", k), n, "z", c_half(p_buf, k), m["c_far", k], c_land(k))
+        sums_2(("c out", k), n, "z", c_half(p_buf, k), m["c_far", k], c_land(k))
 
     def a_scatter_2(k, n):
-        sums_2(("a", k), n, "y", a_half(p_buf, k), m["a_far", k], a_land(k))
+        sums_2(("a out", k), n, "y", a_half(p_buf, k), m["a_far", k], a_land(k))
 
     def b_scatter_2(k, n):
-        sums_2(("b", k), n, "x", b_half(p_buf, k), m["b_far", k], b_land(k))
+        sums_2(("b out", k), n, "x", b_half(p_buf, k), m["b_far", k], b_land(k))
+
+    def rows_half(k, h):
+        return pl.ds(h * (AROWS[k] // 2), AROWS[k] // 2)
+
+    def a_end(k):
+        return (lambda i, h: m["a_sum", k].at[i, rows_half(k, h)], m["a_far2", k],
+                lambda n, h: m["a_in2", k].at[n, rows_half(k, h)])
+
+    def b_end(k):
+        return (lambda i, h: m["b_sum", k].at[rows_half(k, h), cols(i)], m["b_far2", k],
+                lambda n, h: m["b_in2", k].at[n, rows_half(k, h)])
 
     def c_scatter_3(k):
-        arrive(state["c", k][1])
+        arrive(state["c out", k][1])
         c_sum, c_in = m["c_sum", k], m["c_in", k]
         for i in range(RING):
             c_sum[i] = added(p_buf[i, c_rows(k, z), :], [c_in[0, i], c_in[1, i]])
@@ -467,19 +500,31 @@
             state["c", k] = scatter("y", lambda i: c_sum.at[:, :, cols(i)], m["c_in2", k])
 
     def a_scatter_3(k):
-        arrive(state["a", k][1])
+        arrive(state["a out", k][1])
         a_sum, a_in = m["a_sum", k], m["a_in", k]
         for i in range(RING):
             a_sum[i] = added(p_buf[i, a_rows(k), cols(y)], [a_in[0, i], a_in[1, i]])
-        state["a", k] = scatter("x", lambda i: a_sum.at[i], m["a_in2", k])
+        if k in NEAR_OUT:
+            sums_1(("a end", k), (0, 1), "x", *a_end(k))
+        else:
+            state["a end", k] = None, scatter("x", lambda i: a_sum.at[i], m["a_in2", k])
 
     def b_scatter_3(k):
-        arrive(state["b", k][1])
+        arrive(state["b out", k][1])
         b_sum, b_in = m["b_sum", k], m["b_in", k]
         for h in range(0, AROWS[k], 32):
             own = p_buf[x, k * CH + AROWS[k] + h:k * CH + AROWS[k] + h + 32, :]
             b_sum[h:h + 32, :] = added(own, [b_in[0, h:h + 32, :], b_in[1, h:h + 32, :]])
-        state["b", k] = scatter("y", lambda i: b_sum.at[:, cols(i)], m["b_in2", k])
+        if k in NEAR_OUT:
+            sums_1(("b end", k), (0, 1), "y", *b_end(k))
+        else:
+            state["b end", k] = None, scatter("y", lambda i: b_sum.at[:, cols(i)], m["b_in2", k])
+
+    def a_scatter_4(k, n):
+        sums_2(("a end", k), n, "x", *a_end(k))
+
+    def b_scatter_4(k, n):
+        sums_2(("b end", k), n, "y", *b_end(k))
 
     def c_scatter_4(k):
         arrive(state["c", k])
@@ -493,11 +538,11 @@
             state["c", k] = scatter("x", lambda i: c_sum2.at[i], m["c_in3", k])
 
     def ab_scatter_4(k):
-        n, ab = AROWS[k], m["ab", k]
-        arrive(state["a", k])
-        ab[0:n, :] = added(m["a_sum", k][x], [m["a_in2", k][d] for d in range(3)])
-        arrive(state["b", k])
-        ab[n:2 * n, :] = added(m["b_sum", k][:, cols(y)], [m["b_in2", k][d] for d in range(3)])
+        n, ab, parts = AROWS[k], m["ab", k], 2 if k in NEAR_OUT else 3
+        arrive(state["a end", k][1])
+        ab[0:n, :] = added(m["a_sum", k][x], [m["a_in2", k][d] for d in range(parts)])
+        arrive(state["b end", k][1])
+        ab[n:2 * n, :] = added(m["b_sum", k][:, cols(y)], [m["b_in2", k][d] for d in range(parts)])
         state["ab", k] = scatter(
             "z", lambda i: ab.at[pl.ds(pl.multiple_of(i * (n // 2), 16), n // 2), :], m["ab_in", k])
 
@@ -549,29 +594,33 @@
         state["total"] = total
 
     for run, *at in (
-        (c_gather_1, 1), (c_gather_1, 0), (ab_gather_1, 0), (c_gather_1, 2), (c_gather_2, 0), (c_gather_2, 1),
-        (ab_gather_1, 1), (b_gather_2, 0), (a_gather_2, 0), (c_gather_3, 0), (c_gather_2, 2), (ab_gather_1, 2),
-        (c_gather_3, 1), (weights, 0), (b_gather_3, 0, 1), (c_gather_4, 0, 1), (b_gather_3, 0, 0), (tables, 2),
-        (a_gather_3, 0, 1), (a_gather_3, 0, 0), (b_gather_2, 1), (a_gather_2, 1), (c_gather_4, 0, 0),
-        (c_gather_4, 1, 1), (tables, 0), (tables, 1), (c_gather_4, 1, 0), (c_gather_3, 2), (b_gather_3, 1, 0),
-        (b_gather_3, 1, 1), (gathered, 0), (a_gather_3, 1, 0), (a_gather_3, 1, 1), (a_gather_2, 2),
-        (b_gather_2, 2), (scores, 0, 1), (scores, 0, 0), (c_gather_4, 2, 0), (stats, 0), (c_gather_4, 2, 1),
-        (gathered, 1), (b_gather_3, 2, 1), (b_gather_3, 2, 0), (a_gather_3, 2, 0), (a_gather_3, 2, 1),
-        (scores, 1, 0), (scores, 1, 1), (merge_stats, 0, 0), (stats, 1), (gathered, 2), (scores, 2, 0),
-        (merge_stats, 0, 1), (scores, 2, 1), (merge_stats, 1, 0), (stats, 2), (merge_stats, 0, 2),
-        (gradients, 0), (products, 0, 0), (merge_stats, 1, 1), (products, 0, 1), (b_scatter_1, 0),
-        (merge_stats, 2, 0), (a_scatter_1, 0), (c_scatter_1, 0), (merge_stats, 1, 2), (gradients, 1),
-        (products, 1, 1), (merge_stats, 2, 1), (b_scatter_2, 0, 0), (b_scatter_2, 0, 1), (a_scatter_2, 0, 0),
-        (a_scatter_2, 0, 1), (products, 1, 0), (b_scatter_1, 1), (merge_stats, 2, 2), (a_scatter_1, 1),
-        (gradients, 2), (c_scatter_1, 1), (products, 2, 1), (b_scatter_3, 0), (a_scatter_3, 0),
-        (products, 2, 0), (a_scatter_1, 2), (b_scatter_1, 2), (a_scatter_2, 1, 0), (c_scatter_2, 0, 0),
-        (c_scatter_2, 1, 1), (b_scatter_2, 1, 1), (b_scatter_2, 1, 0), (c_scatter_2, 1, 0), (a_scatter_2, 1, 1),
-        (selection, 0), (a_scatter_2, 2, 1), (c_scatter_2, 0, 1), (b_scatter_2, 2, 1), (c_scatter_1, 2),
-        (a_scatter_2, 2, 0), (b_scatter_2, 2, 0), (c_scatter_3, 1), (c_scatter_3, 0), (c_scatter_2, 2, 1),
-        (a_scatter_3, 1), (c_scatter_2, 2, 0), (b_scatter_3, 1), (a_scatter_3, 2), (ab_scatter_4, 0),
-        (b_scatter_3, 2), (c_scatter_3, 2), (c_scatter_4, 0), (c_scatter_4, 1), (ab_scatter_4, 1),
-        (ab_scatter_4, 2), (c_scatter_4, 2), (spread, 0), (spread, 1), (spread, 2), (spread_over, 0),
-        (spread_over, 1), (spread_over, 2), (place_rows, 0), (place_rows, 1), (place_rows, 2),
+        (c_gather_1, 1), (c_gather_1, 0), (ab_gather_1, 0), (ab_gather_1, 1), (c_gather_2, 0), (c_gather_2, 1),
+        (c_gather_1, 2), (tables, 2), (ab_gather_1, 2), (b_gather_2, 0), (b_gather_1, 1, 0), (b_gather_1, 1, 1),
+        (a_gather_2, 0), (tables, 0), (a_gather_1, 1, 1), (a_gather_1, 1, 0), (c_gather_3, 0), (a_gather_1, 2, 0),
+        (b_gather_1, 2, 0), (b_gather_1, 2, 1), (c_gather_3, 1), (weights, 0), (a_gather_1, 2, 1), (b_gather_2, 1),
+        (tables, 1), (a_gather_3, 0, 1), (c_gather_4, 0, 1), (a_gather_3, 0, 0), (c_gather_2, 2), (c_gather_4, 0, 0),
+        (b_gather_3, 0, 0), (b_gather_3, 0, 1), (b_gather_3, 1, 0), (a_gather_2, 1), (b_gather_3, 1, 1),
+        (c_gather_4, 1, 1), (b_gather_2, 2), (a_gather_3, 1, 0), (a_gather_3, 1, 1), (a_gather_2, 2),
+        (c_gather_4, 1, 0), (c_gather_3, 2), (gathered, 0), (scores, 0, 0), (scores, 0, 1), (stats, 0),
+        (b_gather_3, 2, 0), (b_gather_3, 2, 1), (gathered, 1), (a_gather_3, 2, 0), (a_gather_3, 2, 1),
+        (c_gather_4, 2, 1), (scores, 1, 0), (c_gather_4, 2, 0), (scores, 1, 1), (merge_stats, 0, 0), (stats, 1),
+        (gathered, 2), (scores, 2, 0), (merge_stats, 0, 1), (scores, 2, 1), (merge_stats, 1, 0), (stats, 2),
+        (merge_stats, 0, 2), (gradients, 0), (products, 0, 0), (merge_stats, 1, 1), (c_scatter_1, 0, 0),
+        (merge_stats, 2, 0), (a_scatter_1, 0, 0), (products, 0, 1), (c_scatter_1, 0, 1), (a_scatter_1, 0, 1),
+        (b_scatter_1, 0), (merge_stats, 1, 2), (gradients, 1), (products, 1, 1), (merge_stats, 2, 1),
+        (a_scatter_1, 1, 1), (products, 1, 0), (a_scatter_1, 1, 0), (c_scatter_1, 1, 0), (b_scatter_1, 1),
+        (c_scatter_1, 1, 1), (a_scatter_2, 0, 0), (a_scatter_2, 0, 1), (b_scatter_2, 0, 1), (merge_stats, 2, 2),
+        (b_scatter_2, 0, 0), (gradients, 2), (products, 2, 1), (a_scatter_1, 2, 1), (a_scatter_2, 1, 1),
+        (a_scatter_2, 1, 0), (c_scatter_1, 2, 1), (b_scatter_2, 1, 1), (b_scatter_2, 1, 0), (products, 2, 0),
+        (b_scatter_1, 2), (a_scatter_1, 2, 0), (c_scatter_2, 0, 1), (b_scatter_3, 0), (c_scatter_2, 1, 0),
+        (selection, 0), (c_scatter_2, 1, 1), (a_scatter_3, 0), (a_scatter_3, 1), (c_scatter_2, 0, 0),
+        (b_scatter_3, 1), (b_scatter_2, 2, 0), (a_scatter_2, 2, 1), (c_scatter_2, 2, 1), (c_scatter_1, 2, 0),
+        (a_scatter_2, 2, 0), (b_scatter_2, 2, 1), (c_scatter_3, 1), (a_scatter_4, 1, 0), (c_scatter_3, 0),
+        (b_scatter_4, 0, 0), (b_scatter_4, 0, 1), (c_scatter_2, 2, 0), (b_scatter_4, 1, 1), (b_scatter_4, 1, 0),
+        (a_scatter_4, 1, 1), (a_scatter_4, 0, 1), (a_scatter_4, 0, 0), (a_scatter_3, 2), (b_scatter_3, 2),
+        (c_scatter_3, 2), (c_scatter_4, 1), (ab_scatter_4, 0), (c_scatter_4, 0), (ab_scatter_4, 1),
+        (ab_scatter_4, 2), (c_scatter_4, 2), (spread, 0), (spread, 1), (spread, 2), (spread_over, 1),
+        (spread_over, 0), (spread_over, 2), (place_rows, 1), (place_rows, 0), (place_rows, 2),
     ):
         run(*at)
     out[...] = state["total"].astype(BF16)

time: 103 us -> 101 us (0.981)
  Pallas kernels: 100 us -> 98.2 us
    pallas_call x1, Pallas kernels: 100 us -> 98.2 us  [local(): pl.pallas_call(kernel, out_shape=jax.ShapeDtypeStruct((L, DS), BF16), in_...]
where the time goes in v5:
time: 101 us; the launch traced here: 100 us
  Pallas kernels  98.2 us (97%)
  local copies, waits for them, and re-layouts  1.62 us (2%)
    pallas_call x1, Pallas kernels, local(): pl.pallas_call(kernel, out_shape=jax.ShapeDtypeStruct((L, DS), BF16), in_...  98.2 us

profile of v5, /device:TPU:1, one launch (start us, length us, event | category | flops | bytes accessed | tf_op | source)
XLA Modules:
  0.0 100.5 jit_solution(682541091255790217)
XLA Ops:
  0.7 98.2 %masked_row_gradient.1 = bf16[384,256]{1,0:T(8,128)(2,1)} custom-call(bf16[384,256]{1,0:T(8,128)(2,1)} %bitcast.3, s32[1,384]{1,0:T(1,128)} %pos.1, s32[1,384]{1,0:T(1,128)} %tgt.1, s32[1]{0:T(128)S(6)} %copy.7.cnt, bf16[496,4096]{1,0:T(8,128)(2,1)} %w_in.1), custom_call_target="tpu_custom_call" | custom-call | flops 12482248704 | bytes 4063232 | tf_op jit(solution)/shard_map/masked_row_gradient/pallas_call | solution.py:633
  98.9 1.6 %copy.8 = bf16[1,384,256]{2,1,0:T(8,128)(2,1)} copy(bf16[1,384,256]{2,1,0:T(8,128)(2,1)} %bitcast.2) | data formatting | bytes 393216

commit v6 on v5

--- a/solution.py
+++ b/solution.py
@@ -594,33 +594,33 @@
         state["total"] = total
 
     for run, *at in (
-        (c_gather_1, 1), (c_gather_1, 0), (ab_gather_1, 0), (ab_gather_1, 1), (c_gather_2, 0), (c_gather_2, 1),
-        (c_gather_1, 2), (tables, 2), (ab_gather_1, 2), (b_gather_2, 0), (b_gather_1, 1, 0), (b_gather_1, 1, 1),
-        (a_gather_2, 0), (tables, 0), (a_gather_1, 1, 1), (a_gather_1, 1, 0), (c_gather_3, 0), (a_gather_1, 2, 0),
-        (b_gather_1, 2, 0), (b_gather_1, 2, 1), (c_gather_3, 1), (weights, 0), (a_gather_1, 2, 1), (b_gather_2, 1),
-        (tables, 1), (a_gather_3, 0, 1), (c_gather_4, 0, 1), (a_gather_3, 0, 0), (c_gather_2, 2), (c_gather_4, 0, 0),
-        (b_gather_3, 0, 0), (b_gather_3, 0, 1), (b_gather_3, 1, 0), (a_gather_2, 1), (b_gather_3, 1, 1),
-        (c_gather_4, 1, 1), (b_gather_2, 2), (a_gather_3, 1, 0), (a_gather_3, 1, 1), (a_gather_2, 2),
-        (c_gather_4, 1, 0), (c_gather_3, 2), (gathered, 0), (scores, 0, 0), (scores, 0, 1), (stats, 0),
-        (b_gather_3, 2, 0), (b_gather_3, 2, 1), (gathered, 1), (a_gather_3, 2, 0), (a_gather_3, 2, 1),
-        (c_gather_4, 2, 1), (scores, 1, 0), (c_gather_4, 2, 0), (scores, 1, 1), (merge_stats, 0, 0), (stats, 1),
-        (gathered, 2), (scores, 2, 0), (merge_stats, 0, 1), (scores, 2, 1), (merge_stats, 1, 0), (stats, 2),
-        (merge_stats, 0, 2), (gradients, 0), (products, 0, 0), (merge_stats, 1, 1), (c_scatter_1, 0, 0),
-        (merge_stats, 2, 0), (a_scatter_1, 0, 0), (products, 0, 1), (c_scatter_1, 0, 1), (a_scatter_1, 0, 1),
-        (b_scatter_1, 0), (merge_stats, 1, 2), (gradients, 1), (products, 1, 1), (merge_stats, 2, 1),
-        (a_scatter_1, 1, 1), (products, 1, 0), (a_scatter_1, 1, 0), (c_scatter_1, 1, 0), (b_scatter_1, 1),
-        (c_scatter_1, 1, 1), (a_scatter_2, 0, 0), (a_scatter_2, 0, 1), (b_scatter_2, 0, 1), (merge_stats, 2, 2),
-        (b_scatter_2, 0, 0), (gradients, 2), (products, 2, 1), (a_scatter_1, 2, 1), (a_scatter_2, 1, 1),
-        (a_scatter_2, 1, 0), (c_scatter_1, 2, 1), (b_scatter_2, 1, 1), (b_scatter_2, 1, 0), (products, 2, 0),
-        (b_scatter_1, 2), (a_scatter_1, 2, 0), (c_scatter_2, 0, 1), (b_scatter_3, 0), (c_scatter_2, 1, 0),
-        (selection, 0), (c_scatter_2, 1, 1), (a_scatter_3, 0), (a_scatter_3, 1), (c_scatter_2, 0, 0),
-        (b_scatter_3, 1), (b_scatter_2, 2, 0), (a_scatter_2, 2, 1), (c_scatter_2, 2, 1), (c_scatter_1, 2, 0),
-        (a_scatter_2, 2, 0), (b_scatter_2, 2, 1), (c_scatter_3, 1), (a_scatter_4, 1, 0), (c_scatter_3, 0),
-        (b_scatter_4, 0, 0), (b_scatter_4, 0, 1), (c_scatter_2, 2, 0), (b_scatter_4, 1, 1), (b_scatter_4, 1, 0),
-        (a_scatter_4, 1, 1), (a_scatter_4, 0, 1), (a_scatter_4, 0, 0), (a_scatter_3, 2), (b_scatter_3, 2),
-        (c_scatter_3, 2), (c_scatter_4, 1), (ab_scatter_4, 0), (c_scatter_4, 0), (ab_scatter_4, 1),
-        (ab_scatter_4, 2), (c_scatter_4, 2), (spread, 0), (spread, 1), (spread, 2), (spread_over, 1),
-        (spread_over, 0), (spread_over, 2), (place_rows, 1), (place_rows, 0), (place_rows, 2),
+        (c_gather_1, 0), (c_gather_1, 1), (ab_gather_1, 0), (ab_gather_1, 1), (c_gather_1, 2), (c_gather_2, 0),
+        (c_gather_2, 1), (ab_gather_1, 2), (tables, 2), (tables, 0), (b_gather_1, 1, 1), (b_gather_2, 0),
+        (b_gather_1, 1, 0), (a_gather_1, 1, 1), (a_gather_1, 1, 0), (a_gather_2, 0), (c_gather_3, 0),
+        (c_gather_3, 1), (b_gather_1, 2, 0), (weights, 0), (c_gather_2, 2), (b_gather_2, 1), (a_gather_1, 2, 0),
+        (a_gather_1, 2, 1), (b_gather_3, 0, 0), (b_gather_1, 2, 1), (c_gather_4, 0, 0), (a_gather_3, 0, 1),
+        (b_gather_3, 0, 1), (a_gather_3, 0, 0), (a_gather_2, 1), (tables, 1), (b_gather_3, 1, 1), (b_gather_3, 1, 0),
+        (c_gather_4, 0, 1), (a_gather_3, 1, 0), (c_gather_4, 1, 0), (c_gather_4, 1, 1), (b_gather_2, 2),
+        (a_gather_3, 1, 1), (a_gather_2, 2), (c_gather_3, 2), (gathered, 0), (scores, 0, 1), (scores, 0, 0),
+        (stats, 0), (gathered, 1), (scores, 1, 1), (b_gather_3, 2, 1), (a_gather_3, 2, 0), (a_gather_3, 2, 1),
+        (b_gather_3, 2, 0), (c_gather_4, 2, 0), (c_gather_4, 2, 1), (scores, 1, 0), (stats, 1), (merge_stats, 0, 0),
+        (gathered, 2), (scores, 2, 0), (merge_stats, 1, 0), (merge_stats, 0, 1), (scores, 2, 1), (stats, 2),
+        (merge_stats, 1, 1), (merge_stats, 0, 2), (gradients, 0), (products, 0, 1), (c_scatter_1, 0, 1),
+        (merge_stats, 2, 0), (a_scatter_1, 0, 1), (products, 0, 0), (merge_stats, 1, 2), (a_scatter_1, 0, 0),
+        (gradients, 1), (b_scatter_1, 0), (products, 1, 1), (merge_stats, 2, 1), (a_scatter_2, 0, 1),
+        (a_scatter_1, 1, 1), (c_scatter_1, 1, 1), (products, 1, 0), (a_scatter_2, 0, 0), (a_scatter_1, 1, 0),
+        (b_scatter_2, 0, 0), (b_scatter_1, 1), (c_scatter_1, 1, 0), (b_scatter_2, 0, 1), (c_scatter_1, 0, 0),
+        (merge_stats, 2, 2), (gradients, 2), (products, 2, 1), (a_scatter_1, 2, 1), (products, 2, 0),
+        (a_scatter_3, 0), (c_scatter_2, 0, 1), (b_scatter_2, 1, 0), (b_scatter_2, 1, 1), (c_scatter_2, 1, 0),
+        (a_scatter_1, 2, 0), (a_scatter_2, 1, 1), (a_scatter_2, 1, 0), (c_scatter_1, 2, 0), (b_scatter_1, 2),
+        (c_scatter_2, 1, 1), (a_scatter_2, 2, 1), (b_scatter_3, 0), (c_scatter_2, 0, 0), (selection, 0),
+        (a_scatter_4, 0, 1), (c_scatter_1, 2, 1), (b_scatter_3, 1), (a_scatter_2, 2, 0), (a_scatter_4, 0, 0),
+        (a_scatter_3, 1), (b_scatter_2, 2, 0), (b_scatter_4, 0, 0), (b_scatter_2, 2, 1), (c_scatter_2, 2, 0),
+        (c_scatter_3, 1), (c_scatter_3, 0), (b_scatter_4, 0, 1), (b_scatter_4, 1, 0), (c_scatter_2, 2, 1),
+        (a_scatter_3, 2), (b_scatter_4, 1, 1), (b_scatter_3, 2), (a_scatter_4, 1, 1), (a_scatter_4, 1, 0),
+        (c_scatter_3, 2), (c_scatter_4, 0), (ab_scatter_4, 0), (ab_scatter_4, 1), (c_scatter_4, 1),
+        (ab_scatter_4, 2), (c_scatter_4, 2), (spread, 0), (spread, 1), (spread, 2), (spread_over, 0),
+        (spread_over, 1), (spread_over, 2), (place_rows, 1), (place_rows, 0), (place_rows, 2),
     ):
         run(*at)
     out[...] = state["total"].astype(BF16)

time: 101 us -> 101 us (level)
  no operation moved by 1% of the time
where the time goes in v6:
time: 101 us
  Pallas kernels  98.8 us (98%)
  local copies, waits for them, and re-layouts  1.62 us (2%)
    pallas_call x1, Pallas kernels, local(): pl.pallas_call(kernel, out_shape=jax.ShapeDtypeStruct((L, DS), BF16), in_...  98.8 us

profile of v6, /device:TPU:1, one launch (start us, length us, event | category | flops | bytes accessed | tf_op | source)
XLA Modules:
  0.0 101.1 jit_solution(12289226580486803447)
XLA Ops:
  0.7 98.8 %masked_row_gradient.1 = bf16[384,256]{1,0:T(8,128)(2,1)} custom-call(bf16[384,256]{1,0:T(8,128)(2,1)} %bitcast.3, s32[1,384]{1,0:T(1,128)} %pos.1, s32[1,384]{1,0:T(1,128)} %tgt.1, s32[1]{0:T(128)S(6)} %copy.7.cnt, bf16[496,4096]{1,0:T(8,128)(2,1)} %w_in.1), custom_call_target="tpu_custom_call" | custom-call | flops 12482248704 | bytes 4063232 | tf_op jit(solution)/shard_map/masked_row_gradient/pallas_call | solution.py:633
  99.5 1.6 %copy.8 = bf16[1,384,256]{2,1,0:T(8,128)(2,1)} copy(bf16[1,384,256]{2,1,0:T(8,128)(2,1)} %bitcast.2) | data formatting | bytes 393216
